TPU v7x, 256 devices: a whole 4x4x8 slice. The times are simulated.
256 devices in a mesh: fibre: 32 (over z, x_lo, core), win: 8 (over x_hi, y).
Axes of the slice: x: 4 (x_hi: 2, x_lo: 2; x = x_hi * 2 + x_lo), y: 4, z: 8, core: 2. Of those that a mesh axis runs over, the one named last changes fastest.
Arguments:
- raw_segments: bfloat16 [64, 512, 4352], P('win', 'fibre'), may hold values from -6 to 6
- offsets: int32 [64], P('win'), may hold values from 0 to 256, as said below
- channel_mask: int32 [512], P('fibre'), may hold values 0 or 1
Outputs:
- correlations: float32 [128, 512, 512], P('win', 'fibre')
Inputs may be any that keep to these rules, and one draw needn't show every extreme that they name: Window start offsets; 256 occurs in every draw.
All inputs are finite; a program needn't handle non-finite values. No bound on the sum of `channel_mask` on one device may be relied on, other than what follows from the above.
Results may differ from a plain program's by a relative error of at most 0.004.
Values may be sent and summed in bfloat16 or wider, within the bound.
A program may use at most 128 MiB of HBM per device.

v0:
```python
import math

import jax
import jax.numpy as jnp
from jax import lax
from jax.sharding import PartitionSpec as P

RADIX = 64
L = 4096
BAND_LO = 64
NB = 1024
SMOOTH = 64
LAGS = 512
SPAN = 128


EPS = 1e-06


def from_behind(array, axis, by):
    size = lax.axis_size(axis)
    pairs = [(i, i + by) for i in range(size) if 0 <= i + by < size]
    return lax.ppermute(array, axis, pairs)


def hann_taper():
    position = jnp.arange(L, dtype=jnp.float32)
    return 0.5 - 0.5 * jnp.cos(position * (2.0 * math.pi / L))


def lag_table():
    frequency = BAND_LO + jnp.arange(NB, dtype=jnp.int32)
    lag_index = jnp.arange(LAGS, dtype=jnp.int32) - LAGS // 2
    phase_turns = jnp.mod(frequency[:, None] * lag_index[None, :], L)
    angles = phase_turns.astype(jnp.float32) * (2.0 * math.pi / L)
    return jnp.concatenate([jnp.cos(angles), -jnp.sin(angles)], 0).astype(jnp.bfloat16)


def angle_pair(turns, period):
    angles = turns.astype(jnp.float32) * (2.0 * math.pi / period)
    return (jnp.cos(angles), jnp.sin(angles))


def whitened(raw_segments, offsets, channel_mask):
    windows, channels = (raw_segments.shape[0], raw_segments.shape[1])
    taken = jax.vmap(lambda block, begin: lax.dynamic_slice_in_dim(block, begin, L, 1))(
        raw_segments, offsets
    )
    samples = taken.astype(jnp.float32)
    samples = samples - jnp.mean(samples, axis=-1, keepdims=True)
    samples = samples * hann_taper()
    grid = samples.reshape(windows * channels, RADIX, RADIX)
    digits = jnp.arange(RADIX, dtype=jnp.int32)
    cos_first, sin_first = angle_pair(jnp.mod(digits[:, None] * digits[None, :], RADIX), RADIX)
    highest = lax.Precision.HIGHEST
    first_real = jnp.einsum("rab,af->rfb", grid, cos_first, precision=highest)
    first_imag = -jnp.einsum("rab,af->rfb", grid, sin_first, precision=highest)
    cos_twist, sin_twist = angle_pair(jnp.mod(digits[:, None] * digits[None, :], L), L)
    twist_real = first_real * cos_twist + first_imag * sin_twist
    twist_imag = first_imag * cos_twist - first_real * sin_twist
    groups = BAND_LO // RADIX + jnp.arange(NB // RADIX, dtype=jnp.int32)
    cos_second, sin_second = angle_pair(jnp.mod(digits[:, None] * groups[None, :], RADIX), RADIX)
    real_part = jnp.einsum("rfb,bg->rgf", twist_real, cos_second, precision=highest) + jnp.einsum(
        "rfb,bg->rgf", twist_imag, sin_second, precision=highest
    )
    imag_part = jnp.einsum("rfb,bg->rgf", twist_imag, cos_second, precision=highest) - jnp.einsum(
        "rfb,bg->rgf", twist_real, sin_second, precision=highest
    )
    real_part = real_part.reshape(windows, channels, NB)
    imag_part = imag_part.reshape(windows, channels, NB)
    power = (real_part * real_part + imag_part * imag_part).reshape(
        windows, channels, NB // SMOOTH, SMOOTH
    )
    factor = 1.0 / jnp.sqrt(jnp.mean(power, axis=-1) + EPS)
    factor = jnp.repeat(factor, SMOOTH, axis=-1)
    keep = channel_mask.astype(jnp.float32)[None, :, None]
    return (jnp.concatenate([real_part * factor, imag_part * factor], -1) * keep).astype(
        jnp.bfloat16
    )


def partner_block(segment, count, channels):
    return jax.vmap(lambda first: lax.dynamic_slice_in_dim(segment, first, channels, 1))(
        jnp.arange(count, dtype=jnp.int32)
    )


def correlate(own, partners, table, scale):
    half = own.shape[-1] // 2
    own_real = own[..., :half].astype(jnp.float32)
    own_imag = own[..., half:].astype(jnp.float32)
    other_real = partners[..., :half].astype(jnp.float32)
    other_imag = partners[..., half:].astype(jnp.float32)
    cross_real = jnp.sum(own_real * other_real + own_imag * other_imag, axis=1)
    cross_imag = jnp.sum(own_imag * other_real - own_real * other_imag, axis=1)
    cross = jnp.concatenate([cross_real, cross_imag], -1).astype(jnp.bfloat16)
    count, channels = (cross.shape[0], cross.shape[1])
    lagged = jnp.dot(
        cross.reshape(count * channels, 2 * half), table, preferred_element_type=jnp.float32
    )
    return lagged.reshape(count, channels, table.shape[1]) * scale


def body(raw_segments, offsets, channel_mask):
    spectra = whitened(raw_segments, offsets, channel_mask)
    channels = spectra.shape[1]
    reach = SPAN // channels
    pieces = [spectra]
    for step in range(1, reach + 1):
        pieces.append(from_behind(spectra, "fibre", -step))
    extended = jnp.concatenate(pieces, axis=1)
    table = lag_table()
    win_count = lax.axis_size("win")
    scale = 1.0 / math.sqrt(NB * spectra.shape[0] * win_count)
    block_rows = SPAN // win_count

    def one_group(index):
        first = index * block_rows
        segment = lax.dynamic_slice_in_dim(extended, first + 1, channels + block_rows - 1, 1)
        return correlate(spectra, partner_block(segment, block_rows, channels), table, scale)

    results = lax.map(
        one_group, jnp.arange(block_rows * lax.axis_size("win") // block_rows, dtype=jnp.int32)
    )
    return lax.psum_scatter(
        results.reshape(block_rows * lax.axis_size("win"), channels, LAGS),
        "win",
        scatter_dimension=0,
        tiled=True,
    )


def solution(mesh):
    return jax.shard_map(
        body,
        mesh=mesh,
        in_specs=(P("win", "fibre", None), P("win"), P("fibre")),
        out_specs=P("win", "fibre", None),
        check_vma=False,
    )
```

profile of v0, /device:TPU:1, one launch (start us, length us, event | category | flops | bytes accessed | tf_op | source)
XLA Modules:
  0.0 446.0 jit_solution(7682484309371446351)
XLA Ops:
  7.2 23.5 %while.14 = (s32[]{:T(128)}, bf16[8,16,4352]{2,1,0:T(8,128)(2,1)}, s32[8,3]{0,1:T(4,128)S(1)}, bf16[8,16,4096]{2,1,0:T(8,128)(2,1)S(1)}, s32[]{:T(128)}) while((s32[]{:T(128)}, bf16[8,16,4352]{2,1,0:T(8,128)(2,1)}, s32[8,3]{0,1:T(4,128)S(1)}, bf16[8,16,4096]{2,1,0:T(8,128)(2,1)S(1)}, s32[]{:T(128)}) %tuple.53), condition=%wide.while_cond, body=%wide.while_body.sunk | while | flops 2 | bytes 262261 | solution.py:46
  7.9 2.3 dynamic-slice_dynamic-update-slice_fusion.2
  10.8 2.3 dynamic-slice_dynamic-update-slice_fusion.2
  13.8 2.3 dynamic-slice_dynamic-update-slice_fusion.2
  16.7 2.3 dynamic-slice_dynamic-update-slice_fusion.2
  19.6 2.3 dynamic-slice_dynamic-update-slice_fusion.2
  22.6 2.3 dynamic-slice_dynamic-update-slice_fusion.2
  25.5 2.3 dynamic-slice_dynamic-update-slice_fusion.2
  28.5 2.3 dynamic-slice_dynamic-update-slice_fusion.2
  30.7 3.2 reshape.136
  34.7 4.6 %subtract_multiply_fusion = f32[128,64,64]{2,1,0:T(8,128)} fusion(f32[128,64,64]{2,1,0:T(8,128)} %reshape.136, f32[64,64]{1,0:T(8,128)S(1)} %copy.9, f32[128]{0:T(128)S(1)} %div.18), kind=kLoop, calls=%fused_computation.24 | loop fusion | flops 1048576 | bytes 4211200 | tf_op jit(solution)/shard_map/mul | solution.py:51
  39.2 4.7 %copy.10 = f32[128,64,64]{0,1,2:T(8,128)S(1)} copy(f32[128,64,64]{2,1,0:T(8,128)} %subtract_multiply_fusion) | data formatting | bytes 4194304 | tf_op jit(solution)/shard_map/mul | solution.py:51
  43.9 2.1 fusion.47
  46.0 3.2 add_bitcast_fusion
  49.3 2.3 fusion.24
  51.6 2.3 fusion.22
  53.9 2.3 fusion.33
  57.0 3.8 add_reduce_fusion
  64.0 5.1 %collective-permute-start = (bf16[8,16,2048]{2,1,0:T(8,128)(2,1)S(1)}, bf16[8,16,2048]{2,1,0:T(8,128)(2,1)}, u32[]{:S(2)}, u32[]{:S(2)}) collective-permute-start(bf16[8,16,2048]{2,1,0:T(8,128)(2,1)S(1)} %get-tuple-element.120), channel_id=1, source_target_pairs={{8,0},{16,8},{24,16},{32,24},{40,32},{48,40},{56,48},{64,56},{72,6... | collective-permute-start | bytes 1572872 | tf_op jit(solution)/shard_map/ppermute | solution.py:23
  74.4 9.1 %cosine_convert_fusion = (bf16[1024,512]{1,0:T(8,128)(2,1)S(1)}, bf16[1024,512]{1,0:T(8,128)(2,1)S(1)}) fusion(s32[512]{0:T(512)S(1)} %iota_add_fusion.1, s32[1024]{0:T(1024)S(1)} %iota_add_fusion), kind=kLoop, calls=%fused_computation.35 | loop fusion | flops 8912896 | bytes 2103296 | tf_op jit(solution)/shard_map/convert.3
  86.6 1.9 constant_dynamic-update-slice_fusion.7
  90.7 11.6 %collective-permute-done.2 = bf16[8,16,2048]{2,1,0:T(8,128)(2,1)S(1)} collective-permute-done((bf16[8,16,2048]{2,1,0:T(8,128)(2,1)S(1)}, bf16[8,16,2048]{2,1,0:T(8,128)(2,1)S(1)}, u32[]{:S(2)}, u32[]{:S(2)}) %collective-permute-start.2) | collective-permute-done | bytes 524320 | tf_op jit(solution)/shard_map/ppermute | solution.py:23
  104.4 2.3 collective-permute-done.3
  107.6 1.8 collective-permute-done.4
  110.3 2.2 collective-permute-done.5
  113.4 74.5 %collective-permute-done.6 = bf16[8,16,2048]{2,1,0:T(8,128)(2,1)S(1)} collective-permute-done((bf16[8,16,2048]{2,1,0:T(8,128)(2,1)S(1)}, bf16[8,16,2048]{2,1,0:T(8,128)(2,1)S(1)}, u32[]{:S(2)}, u32[]{:S(2)}) %collective-permute-start.6) | collective-permute-done | bytes 524320 | tf_op jit(solution)/shard_map/ppermute | solution.py:23
  188.8 3.6 collective-permute-done.7
  193.2 7.1 %copy.20 = bf16[8,144,2048]{2,0,1:T(8,128)(2,1)} copy(bf16[8,144,2048]{2,1,0:T(8,128)(2,1)} %constant_dynamic-update-slice_fusion) | data formatting | bytes 9437184 | tf_op jit(solution)/shard_map/while | solution.py:122
  200.3 145.1 %while.13 = (s32[]{:T(128)}, f32[8,16,16,512]{3,2,1,0:T(8,128)}, bf16[8,16,2048]{2,0,1:T(8,128)(2,1)S(1)}, s32[8]{0:T(128)S(1)}, bf16[8,144,2048]{2,0,1:T(8,128)...) while((s32[]{:T(128)}, f32[8,16,16,512]{3,2,1,0:T(8,128)}, ...), condition=%wide.region_5.6_spmd, body=%wide.region_2.5_spmd.sunk | while | flops 559808576 | bytes 42927056 | solution.py:122
  202.9 4.9 %gather_fusion = bf16[16,8,16,2048]{3,1,2,0:T(8,128)(2,1)} fusion(bf16[8,31,2048]{2,0,1:T(8,128)(2,1)S(1)} %constant_dynamic-slice_fusion.4, s32[16]{0:T(128)S(1)} %shift-left_bitcast_fusion.2), kind=kCustom, calls=%fused_computation.clone.1 | custom fusion | bytes 16777408 | tf_op jit(solution)/shard_map/while/body/eval_jaxpr/vmap()/gather | solution.py:83
  207.9 9.0 %fusion.119 = (bf16[16,16,1024]{2,1,0:T(8,128)(2,1)S(1)}, bf16[16,16,1024]{2,1,0:T(8,128)(2,1)S(1)}) fusion(f32[8,16,1024]{2,0,1:T(8,128)S(1)} %get-tuple-element.199, f32[8,16,1024]{2,0,1:T(8,128)S(1)} %get-tuple-element.200, bf16[16,8,16,2048]{3,1,2,0:T(8,128)(2,1)} %gather_fusion), kind=kLoop, calls=%fused_computation.8.clone.1 | loop fusion | flops 20447232 | bytes 10485760 | tf_op jit(solution)/shard_map/while/body/eval_jaxpr/reduce_sum | solution.py:94
  216.9 1.5 fusion.120
  221.0 4.9 %gather_fusion = bf16[16,8,16,2048]{3,1,2,0:T(8,128)(2,1)} fusion(bf16[8,31,2048]{2,0,1:T(8,128)(2,1)S(1)} %constant_dynamic-slice_fusion.4, s32[16]{0:T(128)S(1)} %shift-left_bitcast_fusion.2), kind=kCustom, calls=%fused_computation.clone.1 | custom fusion | bytes 16777408 | tf_op jit(solution)/shard_map/while/body/eval_jaxpr/vmap()/gather | solution.py:83
  226.0 9.0 %fusion.119 = (bf16[16,16,1024]{2,1,0:T(8,128)(2,1)S(1)}, bf16[16,16,1024]{2,1,0:T(8,128)(2,1)S(1)}) fusion(f32[8,16,1024]{2,0,1:T(8,128)S(1)} %get-tuple-element.199, f32[8,16,1024]{2,0,1:T(8,128)S(1)} %get-tuple-element.200, bf16[16,8,16,2048]{3,1,2,0:T(8,128)(2,1)} %gather_fusion), kind=kLoop, calls=%fused_computation.8.clone.1 | loop fusion | flops 20447232 | bytes 10485760 | tf_op jit(solution)/shard_map/while/body/eval_jaxpr/reduce_sum | solution.py:94
  239.2 4.9 %gather_fusion = bf16[16,8,16,2048]{3,1,2,0:T(8,128)(2,1)} fusion(bf16[8,31,2048]{2,0,1:T(8,128)(2,1)S(1)} %constant_dynamic-slice_fusion.4, s32[16]{0:T(128)S(1)} %shift-left_bitcast_fusion.2), kind=kCustom, calls=%fused_computation.clone.1 | custom fusion | bytes 16777408 | tf_op jit(solution)/shard_map/while/body/eval_jaxpr/vmap()/gather | solution.py:83
  244.2 9.0 %fusion.119 = (bf16[16,16,1024]{2,1,0:T(8,128)(2,1)S(1)}, bf16[16,16,1024]{2,1,0:T(8,128)(2,1)S(1)}) fusion(f32[8,16,1024]{2,0,1:T(8,128)S(1)} %get-tuple-element.199, f32[8,16,1024]{2,0,1:T(8,128)S(1)} %get-tuple-element.200, bf16[16,8,16,2048]{3,1,2,0:T(8,128)(2,1)} %gather_fusion), kind=kLoop, calls=%fused_computation.8.clone.1 | loop fusion | flops 20447232 | bytes 10485760 | tf_op jit(solution)/shard_map/while/body/eval_jaxpr/reduce_sum | solution.py:94
  257.3 4.9 %gather_fusion = bf16[16,8,16,2048]{3,1,2,0:T(8,128)(2,1)} fusion(bf16[8,31,2048]{2,0,1:T(8,128)(2,1)S(1)} %constant_dynamic-slice_fusion.4, s32[16]{0:T(128)S(1)} %shift-left_bitcast_fusion.2), kind=kCustom, calls=%fused_computation.clone.1 | custom fusion | bytes 16777408 | tf_op jit(solution)/shard_map/while/body/eval_jaxpr/vmap()/gather | solution.py:83
  262.3 9.0 %fusion.119 = (bf16[16,16,1024]{2,1,0:T(8,128)(2,1)S(1)}, bf16[16,16,1024]{2,1,0:T(8,128)(2,1)S(1)}) fusion(f32[8,16,1024]{2,0,1:T(8,128)S(1)} %get-tuple-element.199, f32[8,16,1024]{2,0,1:T(8,128)S(1)} %get-tuple-element.200, bf16[16,8,16,2048]{3,1,2,0:T(8,128)(2,1)} %gather_fusion), kind=kLoop, calls=%fused_computation.8.clone.1 | loop fusion | flops 20447232 | bytes 10485760 | tf_op jit(solution)/shard_map/while/body/eval_jaxpr/reduce_sum | solution.py:94
  275.4 4.9 %gather_fusion = bf16[16,8,16,2048]{3,1,2,0:T(8,128)(2,1)} fusion(bf16[8,31,2048]{2,0,1:T(8,128)(2,1)S(1)} %constant_dynamic-slice_fusion.4, s32[16]{0:T(128)S(1)} %shift-left_bitcast_fusion.2), kind=kCustom, calls=%fused_computation.clone.1 | custom fusion | bytes 16777408 | tf_op jit(solution)/shard_map/while/body/eval_jaxpr/vmap()/gather | solution.py:83
  280.4 9.0 %fusion.119 = (bf16[16,16,1024]{2,1,0:T(8,128)(2,1)S(1)}, bf16[16,16,1024]{2,1,0:T(8,128)(2,1)S(1)}) fusion(f32[8,16,1024]{2,0,1:T(8,128)S(1)} %get-tuple-element.199, f32[8,16,1024]{2,0,1:T(8,128)S(1)} %get-tuple-element.200, bf16[16,8,16,2048]{3,1,2,0:T(8,128)(2,1)} %gather_fusion), kind=kLoop, calls=%fused_computation.8.clone.1 | loop fusion | flops 20447232 | bytes 10485760 | tf_op jit(solution)/shard_map/while/body/eval_jaxpr/reduce_sum | solution.py:94
  293.5 4.9 %gather_fusion = bf16[16,8,16,2048]{3,1,2,0:T(8,128)(2,1)} fusion(bf16[8,31,2048]{2,0,1:T(8,128)(2,1)S(1)} %constant_dynamic-slice_fusion.4, s32[16]{0:T(128)S(1)} %shift-left_bitcast_fusion.2), kind=kCustom, calls=%fused_computation.clone.1 | custom fusion | bytes 16777408 | tf_op jit(solution)/shard_map/while/body/eval_jaxpr/vmap()/gather | solution.py:83
  298.5 9.0 %fusion.119 = (bf16[16,16,1024]{2,1,0:T(8,128)(2,1)S(1)}, bf16[16,16,1024]{2,1,0:T(8,128)(2,1)S(1)}) fusion(f32[8,16,1024]{2,0,1:T(8,128)S(1)} %get-tuple-element.199, f32[8,16,1024]{2,0,1:T(8,128)S(1)} %get-tuple-element.200, bf16[16,8,16,2048]{3,1,2,0:T(8,128)(2,1)} %gather_fusion), kind=kLoop, calls=%fused_computation.8.clone.1 | loop fusion | flops 20447232 | bytes 10485760 | tf_op jit(solution)/shard_map/while/body/eval_jaxpr/reduce_sum | solution.py:94
  307.6 1.5 fusion.120
  311.7 4.9 %gather_fusion = bf16[16,8,16,2048]{3,1,2,0:T(8,128)(2,1)} fusion(bf16[8,31,2048]{2,0,1:T(8,128)(2,1)S(1)} %constant_dynamic-slice_fusion.4, s32[16]{0:T(128)S(1)} %shift-left_bitcast_fusion.2), kind=kCustom, calls=%fused_computation.clone.1 | custom fusion | bytes 16777408 | tf_op jit(solution)/shard_map/while/body/eval_jaxpr/vmap()/gather | solution.py:83
  316.7 9.0 %fusion.119 = (bf16[16,16,1024]{2,1,0:T(8,128)(2,1)S(1)}, bf16[16,16,1024]{2,1,0:T(8,128)(2,1)S(1)}) fusion(f32[8,16,1024]{2,0,1:T(8,128)S(1)} %get-tuple-element.199, f32[8,16,1024]{2,0,1:T(8,128)S(1)} %get-tuple-element.200, bf16[16,8,16,2048]{3,1,2,0:T(8,128)(2,1)} %gather_fusion), kind=kLoop, calls=%fused_computation.8.clone.1 | loop fusion | flops 20447232 | bytes 10485760 | tf_op jit(solution)/shard_map/while/body/eval_jaxpr/reduce_sum | solution.py:94
  329.8 4.9 %gather_fusion = bf16[16,8,16,2048]{3,1,2,0:T(8,128)(2,1)} fusion(bf16[8,31,2048]{2,0,1:T(8,128)(2,1)S(1)} %constant_dynamic-slice_fusion.4, s32[16]{0:T(128)S(1)} %shift-left_bitcast_fusion.2), kind=kCustom, calls=%fused_computation.clone.1 | custom fusion | bytes 16777408 | tf_op jit(solution)/shard_map/while/body/eval_jaxpr/vmap()/gather | solution.py:83
  334.8 9.0 %fusion.119 = (bf16[16,16,1024]{2,1,0:T(8,128)(2,1)S(1)}, bf16[16,16,1024]{2,1,0:T(8,128)(2,1)S(1)}) fusion(f32[8,16,1024]{2,0,1:T(8,128)S(1)} %get-tuple-element.199, f32[8,16,1024]{2,0,1:T(8,128)S(1)} %get-tuple-element.200, bf16[16,8,16,2048]{3,1,2,0:T(8,128)(2,1)} %gather_fusion), kind=kLoop, calls=%fused_computation.8.clone.1 | loop fusion | flops 20447232 | bytes 10485760 | tf_op jit(solution)/shard_map/while/body/eval_jaxpr/reduce_sum | solution.py:94
  345.4 93.7 %reduce-scatter.2.cloned.1.call-done = f32[16,16,512]{2,1,0:T(8,128)} async-done(((f32[128,16,512]{2,1,0:T(8,128)}), f32[16,16,512]{2,1,0:T(8,128)}) %reduce-scatter.2.cloned.1.call-update) | async-done | bytes 524304 | tf_op jit(solution)/shard_map/reduce_scatter | solution.py:125
  (120 shorter events, 52.5 us)
Async XLA Ops:
  6.5 432.6 %reduce-scatter.2.cloned.1.call-start = ((), (), s32[]{:S(2)}) async-start(), calls=%async_computation.1 | async-start | bytes 4718592 | tf_op jit(solution)/shard_map/reduce_scatter | solution.py:125
  49.2 4.6 %copy-start = (f32[128,64,64]{0,1,2:T(8,128)}, f32[128,64,64]{0,1,2:T(8,128)S(1)}, u32[]{:S(2)}) copy-start(f32[128,64,64]{0,1,2:T(8,128)S(1)} %get-tuple-element.125) | copy-start | bytes 6291460
  61.6 1.2 copy-start.2
  64.0 21.3 %collective-permute-start = (bf16[8,16,2048]{2,1,0:T(8,128)(2,1)S(1)}, bf16[8,16,2048]{2,1,0:T(8,128)(2,1)}, u32[]{:S(2)}, u32[]{:S(2)}) collective-permute-start(bf16[8,16,2048]{2,1,0:T(8,128)(2,1)S(1)} %get-tuple-element.120), channel_id=1, source_target_pairs={{8,0},{16,8},{24,16},{32,24},{40,32},{48,40},{56,48},{64,56},{72,6... | collective-permute-start | bytes 1572872 | tf_op jit(solution)/shard_map/ppermute | solution.py:23
  69.2 19.4 %collective-permute-start.1 = (bf16[8,16,2048]{2,1,0:T(8,128)(2,1)S(1)}, bf16[8,16,2048]{2,1,0:T(8,128)(2,1)S(1)}, u32[]{:S(2)}, u32[]{:S(2)}) collective-permute-start(bf16[8,16,2048]{2,1,0:T(8,128)(2,1)S(1)} %get-tuple-element.120), channel_id=1, source_target_pairs={{16,0},{24,8},{32,16},{40,24},{48,32},{56,40},{64,48},{72,56},{80,... | collective-permute-start | bytes 1572872 | tf_op jit(solution)/shard_map/ppermute | solution.py:23
  70.5 31.8 %collective-permute-start.2 = (bf16[8,16,2048]{2,1,0:T(8,128)(2,1)S(1)}, bf16[8,16,2048]{2,1,0:T(8,128)(2,1)S(1)}, u32[]{:S(2)}, u32[]{:S(2)}) collective-permute-start(bf16[8,16,2048]{2,1,0:T(8,128)(2,1)S(1)} %get-tuple-element.120), channel_id=1, source_target_pairs={{24,0},{32,8},{40,16},{48,24},{56,32},{64,40},{72,48},{80,56},{88,... | collective-permute-start | bytes 1572872 | tf_op jit(solution)/shard_map/ppermute | solution.py:23
  71.8 35.0 %collective-permute-start.3 = (bf16[8,16,2048]{2,1,0:T(8,128)(2,1)S(1)}, bf16[8,16,2048]{2,1,0:T(8,128)(2,1)S(1)}, u32[]{:S(2)}, u32[]{:S(2)}) collective-permute-start(bf16[8,16,2048]{2,1,0:T(8,128)(2,1)S(1)} %get-tuple-element.120), channel_id=1, source_target_pairs={{32,0},{40,8},{48,16},{56,24},{64,32},{72,40},{80,48},{88,56},{96,... | collective-permute-start | bytes 1572872 | tf_op jit(solution)/shard_map/ppermute | solution.py:23
  73.1 36.4 %collective-permute-start.4 = (bf16[8,16,2048]{2,1,0:T(8,128)(2,1)S(1)}, bf16[8,16,2048]{2,1,0:T(8,128)(2,1)S(1)}, u32[]{:S(2)}, u32[]{:S(2)}) collective-permute-start(bf16[8,16,2048]{2,1,0:T(8,128)(2,1)S(1)} %get-tuple-element.120), channel_id=1, source_target_pairs={{40,0},{48,8},{56,16},{64,24},{72,32},{80,40},{88,48},{96,56},{104... | collective-permute-start | bytes 1572872 | tf_op jit(solution)/shard_map/ppermute | solution.py:23
  85.3 27.2 %collective-permute-start.5 = (bf16[8,16,2048]{2,1,0:T(8,128)(2,1)S(1)}, bf16[8,16,2048]{2,1,0:T(8,128)(2,1)S(1)}, u32[]{:S(2)}, u32[]{:S(2)}) collective-permute-start(bf16[8,16,2048]{2,1,0:T(8,128)(2,1)S(1)} %get-tuple-element.120), channel_id=1, source_target_pairs={{48,0},{56,8},{64,16},{72,24},{80,32},{88,40},{96,48},{104,56},{11... | collective-permute-start | bytes 1572872 | tf_op jit(solution)/shard_map/ppermute | solution.py:23
  88.5 99.4 %collective-permute-start.6 = (bf16[8,16,2048]{2,1,0:T(8,128)(2,1)S(1)}, bf16[8,16,2048]{2,1,0:T(8,128)(2,1)S(1)}, u32[]{:S(2)}, u32[]{:S(2)}) collective-permute-start(bf16[8,16,2048]{2,1,0:T(8,128)(2,1)S(1)} %get-tuple-element.120), channel_id=1, source_target_pairs={{56,0},{64,8},{72,16},{80,24},{88,32},{96,40},{104,48},{112,56},{1... | collective-permute-start | bytes 1572872 | tf_op jit(solution)/shard_map/ppermute | solution.py:23
  102.3 90.1 %collective-permute-start.7 = (bf16[8,16,2048]{2,1,0:T(8,128)(2,1)S(1)}, bf16[8,16,2048]{2,1,0:T(8,128)(2,1)S(1)}, u32[]{:S(2)}, u32[]{:S(2)}) collective-permute-start(bf16[8,16,2048]{2,1,0:T(8,128)(2,1)S(1)} %get-tuple-element.120), channel_id=1, source_target_pairs={{64,0},{72,8},{80,16},{88,24},{96,32},{104,40},{112,48},{120,56},{... | collective-permute-start | bytes 1572872 | tf_op jit(solution)/shard_map/ppermute | solution.py:23
  207.9 9.1 %copy-start.1 = (bf16[2048,512]{1,0:T(8,128)(2,1)S(1)}, bf16[2048,512]{1,0:T(8,128)(2,1)}, u32[]{:S(2)}) copy-start(bf16[2048,512]{1,0:T(8,128)(2,1)} %get-tuple-element.251) | copy-start | bytes 6291460 | tf_op jit(solution)/shard_map/while
  226.0 9.1 %copy-start.1 = (bf16[2048,512]{1,0:T(8,128)(2,1)S(1)}, bf16[2048,512]{1,0:T(8,128)(2,1)}, u32[]{:S(2)}) copy-start(bf16[2048,512]{1,0:T(8,128)(2,1)} %get-tuple-element.251) | copy-start | bytes 6291460 | tf_op jit(solution)/shard_map/while
  244.2 9.1 %copy-start.1 = (bf16[2048,512]{1,0:T(8,128)(2,1)S(1)}, bf16[2048,512]{1,0:T(8,128)(2,1)}, u32[]{:S(2)}) copy-start(bf16[2048,512]{1,0:T(8,128)(2,1)} %get-tuple-element.251) | copy-start | bytes 6291460 | tf_op jit(solution)/shard_map/while
  262.3 9.1 %copy-start.1 = (bf16[2048,512]{1,0:T(8,128)(2,1)S(1)}, bf16[2048,512]{1,0:T(8,128)(2,1)}, u32[]{:S(2)}) copy-start(bf16[2048,512]{1,0:T(8,128)(2,1)} %get-tuple-element.251) | copy-start | bytes 6291460 | tf_op jit(solution)/shard_map/while
  280.4 9.1 %copy-start.1 = (bf16[2048,512]{1,0:T(8,128)(2,1)S(1)}, bf16[2048,512]{1,0:T(8,128)(2,1)}, u32[]{:S(2)}) copy-start(bf16[2048,512]{1,0:T(8,128)(2,1)} %get-tuple-element.251) | copy-start | bytes 6291460 | tf_op jit(solution)/shard_map/while
  298.5 9.1 %copy-start.1 = (bf16[2048,512]{1,0:T(8,128)(2,1)S(1)}, bf16[2048,512]{1,0:T(8,128)(2,1)}, u32[]{:S(2)}) copy-start(bf16[2048,512]{1,0:T(8,128)(2,1)} %get-tuple-element.251) | copy-start | bytes 6291460 | tf_op jit(solution)/shard_map/while
  316.7 9.1 %copy-start.1 = (bf16[2048,512]{1,0:T(8,128)(2,1)S(1)}, bf16[2048,512]{1,0:T(8,128)(2,1)}, u32[]{:S(2)}) copy-start(bf16[2048,512]{1,0:T(8,128)(2,1)} %get-tuple-element.251) | copy-start | bytes 6291460 | tf_op jit(solution)/shard_map/while
  334.8 9.1 %copy-start.1 = (bf16[2048,512]{1,0:T(8,128)(2,1)S(1)}, bf16[2048,512]{1,0:T(8,128)(2,1)}, u32[]{:S(2)}) copy-start(bf16[2048,512]{1,0:T(8,128)(2,1)} %get-tuple-element.251) | copy-start | bytes 6291460 | tf_op jit(solution)/shard_map/while
Sparse Core Ops, SparseCore 0:
  345.6 93.5 reduce-scatter.1
where the time goes:
time: 447 us; the launch traced here: 446 us
  waiting for transfers between devices  190 us (43%)
  local copies, waits for them, and re-layouts  104 us (23%)
  other arithmetic  90.8 us (20%)
  matrix products  28.2 us (6%)
  starting transfers between devices  14.1 us (3%)
  between operations  13.7 us (3%)
  loops' own time  5.67 us (1%)
    ppermute x8, waiting for transfers between devices, from_behind(): return lax.ppermute(array, axis, pairs)  96.1 us
    reduce_scatter x1, waiting for transfers between devices, body(): lax.psum_scatter(results.reshape(block_rows * lax.axis_size('win'), chann...  93.7 us
    reduce_sum x8, other arithmetic, correlate(): cross_real = jnp.sum(own_real * other_real + own_imag * other_imag, axis=1)  72.4 us
    gather x8, local copies, waits for them, and re-layouts, partner_block(): lax.dynamic_slice_in_dim(segment, first, channels, 1)  39 us
    gather x24, local copies, waits for them, and re-layouts  23.4 us
    ppermute x8, starting transfers between devices, from_behind(): return lax.ppermute(array, axis, pairs)  14.1 us
    dot_general x8, matrix products, correlate(): jnp.dot(cross.reshape(count * channels, 2 * half), table, preferred_eleme...  12.2 us
    dynamic_slice x8, local copies, waits for them, and re-layouts, one_group(): lax.dynamic_slice_in_dim(extended, first + 1, channels + block_rows - 1, 1)  10.3 us
  transfers between devices with their start and end apart: 9, of which 7 were waited for; matrix products, arithmetic and copies ran while one was open for 4% of the time, Pallas kernels for 0%

commit v1 on v0

v1 whole, which is shorter than its diff:
```python
import functools
import math

import jax
import jax.numpy as jnp
import numpy as np
from jax import lax
from jax.experimental import pallas as pl
from jax.experimental.pallas import tpu as pltpu
from jax.sharding import PartitionSpec as P

MESH = pl.DeviceIdType.MESH
L = 4096
BAND_LO = 64
NB = 1024
SMOOTH = 64
LAGS = 512
SPAN = 128
EPS = 1e-06
RADIX = 16
TAIL = L // RADIX
PLANE = 32
WIN = 8
QUAD = 4
BINS = 32
F32 = jnp.float32
BF16 = jnp.bfloat16


def second_stage():
    b = np.arange(TAIL)[:, None]
    lane = np.arange(128)[None, :]
    half, imag, low = lane // 64, (lane // 32) % 2, lane % 32
    angle = 2.0 * np.pi * ((b * (BAND_LO // RADIX + half * 32 + low)) % TAIL) / TAIL
    cos, sin = np.cos(angle), np.sin(angle)
    real = np.concatenate([cos, sin], 0)
    imaginary = np.concatenate([-sin, cos], 0)
    pick = np.concatenate([imag, imag], 1) == 0
    straight = np.where(imag == 0, real, imaginary)
    turned = np.where(imag == 0, -imaginary, real)
    del pick
    whole = np.concatenate([straight, turned], 1).astype(np.float32)
    high = whole.astype(jnp.bfloat16)
    low_part = (whole - high.astype(np.float32)).astype(jnp.bfloat16)
    return high, low_part


def twiddles():
    f = np.arange(RADIX)[:, None]
    b = np.arange(TAIL)[None, :]
    angle = 2.0 * np.pi * (f * b) / L
    return np.cos(angle).astype(np.float32), np.sin(angle).astype(np.float32)


def lag_rows():
    frequency = np.arange(NB, dtype=np.int64) + BAND_LO
    lag_index = np.arange(LAGS, dtype=np.int64) - LAGS // 2
    turns = np.mod(frequency[:, None] * lag_index[None, :], L).astype(np.float32)
    angles = turns * np.float32(2.0 * math.pi / L)
    cos, sin = np.cos(angles.astype(np.float64)), np.sin(angles.astype(np.float64))
    table = np.stack([cos, -sin], 1).astype(np.float32)
    bins = RADIX * np.arange(64)[None, :] + np.arange(RADIX)[:, None]
    return table[bins].reshape(2 * NB, LAGS).astype(jnp.bfloat16)


def real_fft(x):
    n = len(x)
    if n == 2:
        return [(x[0] + x[1], None), (x[0] - x[1], None)]
    even, odd = real_fft(x[0::2]), real_fft(x[1::2])
    half, quarter = n // 2, n // 4
    out = [None] * (half + 1)
    out[0] = (even[0][0] + odd[0][0], None)
    out[half] = (even[0][0] - odd[0][0], None)
    for k in range(1, quarter):
        (er, ei), (orr, oi) = even[k], odd[k]
        c, s = math.cos(2.0 * math.pi * k / n), math.sin(2.0 * math.pi * k / n)
        if 8 * k == n:
            tr, ti = (orr + oi) * c, (oi - orr) * c
        else:
            tr, ti = orr * c + oi * s, oi * c - orr * s
        out[k] = (er + tr, ei + ti)
        out[half - k] = (er - tr, ti - ei)
    out[quarter] = (even[quarter][0], -odd[quarter][0])
    return out


def transform_kernel(offsets, raw, keep, tw_cos, tw_sin, w_hi, w_lo, out, lhs, kept, phase_cos, phase_sin):
    def one_window(w, carry):
        off = offsets[w]
        u = lax.broadcasted_iota(jnp.int32, (RADIX, TAIL), 0) * TAIL + lax.broadcasted_iota(
            jnp.int32, (RADIX, TAIL), 1
        )
        taper = 0.5 - 0.5 * jnp.cos(((u - off) & (L - 1)).astype(F32) * (2.0 * math.pi / L))
        f = lax.broadcasted_iota(jnp.int32, (RADIX, 128), 0)
        lane = lax.broadcasted_iota(jnp.int32, (RADIX, 128), 1)
        k = (BAND_LO // RADIX + (lane // 64) * 32 + lane % 32) * RADIX + f
        angle = ((k * off) & (L - 1)).astype(F32) * (2.0 * math.pi / L)
        phase_cos[w] = jnp.cos(angle)
        phase_sin[w] = jnp.sin(angle)
        samples = raw[w].astype(F32)
        first = jnp.where(
            lax.broadcasted_iota(jnp.int32, (16, TAIL), 1) < off, samples[:, L : L + TAIL], samples[:, :TAIL]
        )
        tiles = [first] + [samples[:, a * TAIL : (a + 1) * TAIL] for a in range(1, RADIX)]
        total = functools.reduce(lambda p, q: p + q, tiles)
        mean = jnp.sum(total, axis=1, keepdims=True) * (1.0 / L)
        tiles = [(tile - mean) * taper[a : a + 1, :] for a, tile in enumerate(tiles)]
        spectrum = real_fft(tiles)
        rows = pl.ds(pl.multiple_of(w * 16, 16), 16)
        for f in range(RADIX):
            re, im = spectrum[f] if f <= RADIX // 2 else spectrum[RADIX - f]
            if f > RADIX // 2:
                im = -im
            if f:
                c, s = tw_cos[f : f + 1, :], tw_sin[f : f + 1, :]
                re, im = (re * c, -re * s) if im is None else (re * c + im * s, im * c - re * s)
            else:
                im = jnp.zeros_like(re)
            for part, value in enumerate((re, im)):
                high = value.astype(BF16)
                lhs[f, rows, part * TAIL : (part + 1) * TAIL] = high
                lhs[f, rows, (2 + part) * TAIL : (3 + part) * TAIL] = (value - high.astype(F32)).astype(BF16)
        return carry

    lax.fori_loop(0, 8, one_window, 0)

    def one_column(f, power):
        high, low = lhs[f, :, : 2 * TAIL], lhs[f, :, 2 * TAIL :]
        both = (
            jnp.dot(high, w_hi[...], preferred_element_type=F32)
            + jnp.dot(high, w_lo[...], preferred_element_type=F32)
            + jnp.dot(low, w_hi[...], preferred_element_type=F32)
        ).reshape(8, 16, 256)
        c = phase_cos[:, pl.ds(f, 1), :]
        s = phase_sin[:, pl.ds(f, 1), :]
        value = (both[:, :, :128] * c + both[:, :, 128:] * s).reshape(128, 128)
        kept[f] = value
        return power + value * value

    power = lax.fori_loop(0, RADIX, one_column, jnp.zeros((128, 128), F32))
    row = lax.broadcasted_iota(jnp.int32, (128, 128), 0)
    col = lax.broadcasted_iota(jnp.int32, (128, 128), 1)
    same = (row // 64 == col // 64) & ((row % 32) // 4 == (col % 32) // 4)
    block = jnp.where(same, 1.0, 0.0).astype(F32)
    mean_power = jnp.dot(power, block, precision=lax.Precision.HIGHEST, preferred_element_type=F32) * (1.0 / SMOOTH)
    flag = jnp.broadcast_to(keep[...].astype(F32)[None], (8, 16, 1)).reshape(128, 1)
    factor = (1.0 / jnp.sqrt(mean_power + EPS)) * flag
    left = lax.broadcasted_iota(jnp.int32, (64, 128), 1) < 64

    def one_store(f, carry):
        value = kept[f] * factor
        top, bottom = value[:64], value[64:]
        out[2 * f] = jnp.where(left, top, pltpu.roll(bottom, 64, 1)).astype(BF16)
        out[2 * f + 1] = jnp.where(left, pltpu.roll(top, 64, 1), bottom).astype(BF16)
        return carry

    lax.fori_loop(0, RADIX, one_store, 0)


def transform(raw, offsets, mask):
    w_hi, w_lo = second_stage()
    tw_cos, tw_sin = twiddles()
    vmem = pl.BlockSpec(memory_space=pltpu.VMEM)
    return pl.pallas_call(
        transform_kernel,
        out_shape=jax.ShapeDtypeStruct((PLANE, 64, 128), BF16),
        in_specs=[pl.BlockSpec(memory_space=pltpu.SMEM)] + [vmem] * 6,
        out_specs=vmem,
        scratch_shapes=[
            pltpu.VMEM((RADIX, 128, 4 * TAIL), BF16),
            pltpu.VMEM((RADIX, 128, 128), F32),
            pltpu.VMEM((8, RADIX, 128), F32),
            pltpu.VMEM((8, RADIX, 128), F32),
        ],
        compiler_params=pltpu.CompilerParams(vmem_limit_bytes=40 * 2**20),
        name="transform",
    )(offsets, raw, mask.reshape(16, 1), tw_cos, tw_sin, w_hi, w_lo)


def place():
    fibre, win = lax.axis_index("fibre"), lax.axis_index("win")
    return fibre // QUAD, win * QUAD + fibre % QUAD


def device(z, s):
    return (z * QUAD + s % QUAD, s // QUAD)


def plane_exchange_kernel(send, recv, send_sem, recv_sem, own_sem):
    z, me = place()
    barrier = pltpu.get_barrier_semaphore()

    def greet(j, carry):
        pl.semaphore_signal(barrier, inc=1, device_id=device(z, (me + j) % PLANE), device_id_type=MESH)
        return carry

    lax.fori_loop(1, PLANE, greet, 0)
    own = pltpu.make_async_copy(send.at[me], recv.at[me], own_sem)
    own.start()
    pl.semaphore_wait(barrier, PLANE - 1)

    def copy(j):
        to = (me + j) % PLANE
        return pltpu.make_async_remote_copy(
            src_ref=send.at[to],
            dst_ref=recv.at[me],
            send_sem=send_sem.at[j],
            recv_sem=recv_sem.at[j],
            device_id=device(z, to),
            device_id_type=MESH,
        )

    def start(j, carry):
        copy(j).start()
        return carry

    def finish(j, carry):
        copy(j).wait()
        return carry

    lax.fori_loop(1, PLANE, start, 0)
    lax.fori_loop(1, PLANE, finish, 0)
    own.wait()


def plane_exchange(send, collective_id, name):
    vmem = pl.BlockSpec(memory_space=pltpu.VMEM)
    return pl.pallas_call(
        plane_exchange_kernel,
        out_shape=jax.ShapeDtypeStruct(send.shape, send.dtype),
        in_specs=[vmem],
        out_specs=vmem,
        scratch_shapes=[
            pltpu.SemaphoreType.DMA((PLANE,)),
            pltpu.SemaphoreType.DMA((PLANE,)),
            pltpu.SemaphoreType.DMA,
        ],
        compiler_params=pltpu.CompilerParams(
            collective_id=collective_id, has_side_effects=True, vmem_limit_bytes=16 * 2**20
        ),
        name=name,
    )(send)


def halo_kernel(planes, own, halo, send_sem, recv_sem):
    z, me = place()
    barrier = pltpu.get_barrier_semaphore()
    for step in (1, 2):
        for to in (z + step, z + planes - step):
            pl.semaphore_signal(barrier, inc=1, device_id=device(to % planes, me), device_id_type=MESH)
    pl.semaphore_wait(barrier, 4)
    copies = [
        pltpu.make_async_remote_copy(
            src_ref=own,
            dst_ref=halo.at[step],
            send_sem=send_sem.at[step],
            recv_sem=recv_sem.at[step],
            device_id=device((z + planes - 1 - step) % planes, me),
            device_id_type=MESH,
        )
        for step in (0, 1)
    ]
    for copy in copies:
        copy.start()
    for copy in copies:
        copy.wait()


def halo_exchange(own, planes):
    vmem = pl.BlockSpec(memory_space=pltpu.VMEM)
    return pl.pallas_call(
        functools.partial(halo_kernel, planes),
        out_shape=jax.ShapeDtypeStruct((2,) + own.shape, own.dtype),
        in_specs=[vmem],
        out_specs=vmem,
        scratch_shapes=[pltpu.SemaphoreType.DMA((2,)), pltpu.SemaphoreType.DMA((2,))],
        compiler_params=pltpu.CompilerParams(
            collective_id=1, has_side_effects=True, vmem_limit_bytes=16 * 2**20
        ),
        name="halo",
    )(own)


def relayout_kernel(recv, own, turned):
    def one(index, carry):
        v, w = index // 2, index % 2
        parts = [
            recv[v * QUAD + q, pl.ds(pl.multiple_of((p * 2 + w) * 16, 16), 16), :]
            for p in range(2)
            for q in range(QUAD)
        ]
        block = jnp.concatenate([part.astype(F32) for part in parts], 0)
        turned[pl.ds(pl.multiple_of(index * 128, 128), 128), :] = block.T
        return carry

    lax.fori_loop(0, 16, one, 0)

    def gather(g, carry):
        real = turned[pl.ds(g, 32, stride=64), :]
        imag = turned[pl.ds(32 + g, 32, stride=64), :]
        own[g] = jnp.concatenate([real, imag], 0).astype(BF16)
        return carry

    lax.fori_loop(0, BINS, gather, 0)


def relayout(recv):
    vmem = pl.BlockSpec(memory_space=pltpu.VMEM)
    return pl.pallas_call(
        relayout_kernel,
        out_shape=jax.ShapeDtypeStruct((BINS, 64, 128), BF16),
        in_specs=[vmem],
        out_specs=vmem,
        scratch_shapes=[pltpu.VMEM((2048, 128), F32)],
        compiler_params=pltpu.CompilerParams(vmem_limit_bytes=16 * 2**20),
        name="relayout",
    )(recv)


def cross_kernel(planes, own, halo, out, near, far, column):
    z, _ = place()
    left = lax.broadcasted_iota(jnp.int32, (64, 128), 1) < 64

    def one_bin(g, carry):
        a = own[g].astype(F32)
        e1 = jnp.where(z + 1 < planes, halo[0, g].astype(F32), 0.0)
        e2 = jnp.where(z + 2 < planes, halo[1, g].astype(F32), 0.0)
        b = jnp.concatenate([a[32:], -a[:32]], 0)
        ra, rb, r1, r2 = (pltpu.roll(x, 64, 1) for x in (a, b, e1, e2))
        lhs = jnp.concatenate([jnp.where(left, a, rb), jnp.where(left, ra, b)], 0)
        rhs = jnp.concatenate([jnp.where(left, a, r1), jnp.where(left, ra, e1)], 0)
        last = jnp.concatenate([e2, r2], 0)
        lhs = lhs.T.astype(BF16)
        rows = pl.ds(pl.multiple_of(g * 128, 128), 128)
        near[rows, :] = jnp.dot(lhs, rhs.astype(BF16), preferred_element_type=F32)
        far[rows, :] = jnp.dot(lhs, last.astype(BF16), preferred_element_type=F32)
        return carry

    lax.fori_loop(0, BINS, one_bin, 0)
    wide = lax.broadcasted_iota(jnp.int32, (128, 128), 1) < 64

    def one_pair(index, carry):
        q, i = index // 8, index % 8
        c = q * 16 + i
        for part, ref in enumerate((near, far)):
            block = jnp.concatenate([ref[pl.ds(c, 64, stride=64), :], ref[pl.ds(c + 8, 64, stride=64), :]], 0)
            column[part * 128 : (part + 1) * 128, :] = block.T
        value = jnp.where(wide, column[pl.ds(c + 1, 128), :], column[pl.ds(c + 9, 128), :]).astype(BF16)
        for v in range(WIN):
            out[v * QUAD + q, pl.ds(pl.multiple_of(i * 16, 16), 16), :] = value[v * 16 : (v + 1) * 16]
        return carry

    lax.fori_loop(0, 32, one_pair, 0)


def cross(own, halo, planes):
    vmem = pl.BlockSpec(memory_space=pltpu.VMEM)
    return pl.pallas_call(
        functools.partial(cross_kernel, planes),
        out_shape=jax.ShapeDtypeStruct((PLANE, 128, 128), BF16),
        in_specs=[vmem, vmem],
        out_specs=vmem,
        scratch_shapes=[pltpu.VMEM((4096, 128), F32), pltpu.VMEM((4096, 128), F32), pltpu.VMEM((256, 128), F32)],
        compiler_params=pltpu.CompilerParams(vmem_limit_bytes=32 * 2**20),
        name="cross",
    )(own, halo)


def lag_kernel(scale, spectra, table, out, lhs):
    left = lax.broadcasted_iota(jnp.int32, (128, 128), 1) < 64
    for f in range(RADIX):
        one, two = spectra[2 * f].astype(F32), spectra[2 * f + 1].astype(F32)
        lhs[:128, f * 128 : (f + 1) * 128] = jnp.where(left, one, pltpu.roll(two, 64, 1)).astype(BF16)
        lhs[128:, f * 128 : (f + 1) * 128] = jnp.where(left, pltpu.roll(one, 64, 1), two).astype(BF16)
    for part in range(LAGS // 128):
        lags = jnp.dot(lhs[...], table[:, part * 128 : (part + 1) * 128], preferred_element_type=F32) * scale
        for c in range(16):
            out[part, pl.ds(c, 16, stride=16), :] = lags[c * 16 : (c + 1) * 16]


def lag_transform(spectra, scale):
    vmem = pl.BlockSpec(memory_space=pltpu.VMEM)
    out = pl.pallas_call(
        functools.partial(lag_kernel, scale),
        out_shape=jax.ShapeDtypeStruct((4, 256, 128), F32),
        in_specs=[vmem, vmem],
        out_specs=vmem,
        scratch_shapes=[pltpu.VMEM((256, 2 * NB), BF16)],
        compiler_params=pltpu.CompilerParams(vmem_limit_bytes=32 * 2**20),
        name="lags",
    )(spectra, lag_rows())
    return out.transpose(1, 0, 2).reshape(16, 16, LAGS)


def body(planes, raw, offsets, mask):
    sent = transform(raw, offsets, mask)
    own = relayout(plane_exchange(sent, 0, "to_bins"))
    halo = halo_exchange(own, planes)
    spectra = plane_exchange(cross(own, halo, planes), 2, "to_offsets")
    return lag_transform(spectra, 1.0 / math.sqrt(NB * 8 * WIN))


def solution(mesh):
    planes = mesh.shape["fibre"] // QUAD
    return jax.shard_map(
        functools.partial(body, planes),
        mesh=mesh,
        in_specs=(P("win", "fibre", None), P("win"), P("fibre")),
        out_specs=P("win", "fibre", None),
        check_vma=False,
    )
```

time: 447 us -> 115 us (0.26)
  waiting for transfers between devices: 190 us -> 0 us
  Pallas kernels: 0 us -> 107 us
  local copies, waits for them, and re-layouts: 104 us -> 7.32 us
  other arithmetic: 90.8 us -> 0 us
  matrix products: 28.2 us -> 0 us
  starting transfers between devices: 14.1 us -> 0 us
  between operations: 13.7 us -> 0.08 us
  loops' own time: 5.67 us -> 0 us
    pallas_call x0 -> x7, Pallas kernels: none -> 107 us  [the longest x1 41.5 us: halo_exchange(): pl.pallas_call(functools.partial(halo_kernel, planes), out_shape=jax.Shap...]
    ppermute x8 -> x0, waiting for transfers between devices: 96.1 us -> none  [from_behind(): return lax.ppermute(array, axis, pairs)]
    reduce_scatter x1 -> x0, waiting for transfers between devices: 93.7 us -> none  [body(): lax.psum_scatter(results.reshape(block_rows * lax.axis_size('win'), chann...]
    reduce_sum x9 -> x0, other arithmetic: 72.6 us -> none  [the longest x8 72.4 us: correlate(): cross_real = jnp.sum(own_real * other_real + own_imag * other_imag, axis=1)]
    gather x32 -> x0, local copies, waits for them, and re-layouts: 62.4 us -> none  [the longest x8 39 us: partner_block(): lax.dynamic_slice_in_dim(segment, first, channels, 1)]
    dot_general x14 -> x0, matrix products: 28.2 us -> none  [the longest x8 12.2 us: correlate(): jnp.dot(cross.reshape(count * channels, 2 * half), table, preferred_eleme...]
    dynamic_slice x16 -> x0, local copies, waits for them, and re-layouts: 15.1 us -> none  [the longest x8 10.3 us: one_group(): lax.dynamic_slice_in_dim(extended, first + 1, channels + block_rows - 1, 1)]
    ppermute x8 -> x0, starting transfers between devices: 14.1 us -> none  [from_behind(): return lax.ppermute(array, axis, pairs)]
  transfers between devices with their start and end apart: 9 -> 0, of which waited for: 7 -> 0; matrix products, arithmetic and copies ran while one was open for 4% -> 0% of each run, Pallas kernels for 0% -> 0%
where the time goes in v1:
time: 115 us; the launch traced here: 114 us
  Pallas kernels  107 us (93%)
  local copies, waits for them, and re-layouts  7.32 us (6%)
    pallas_call x1, Pallas kernels, halo_exchange(): pl.pallas_call(functools.partial(halo_kernel, planes), out_shape=jax.Shap...  41.5 us
    pallas_call x2, Pallas kernels, plane_exchange(): pl.pallas_call(plane_exchange_kernel, out_shape=jax.ShapeDtypeStruct(send...  36.5 us
    pallas_call x1, Pallas kernels, cross(): pl.pallas_call(functools.partial(cross_kernel, planes), out_shape=jax.Sha...  15.7 us
    pallas_call x1, Pallas kernels, transform(): pl.pallas_call(transform_kernel, out_shape=jax.ShapeDtypeStruct((PLANE, 6...  8.97 us
    unnamed x14, local copies, waits for them, and re-layouts  5.24 us
    pallas_call x1, Pallas kernels, relayout(): pl.pallas_call(relayout_kernel, out_shape=jax.ShapeDtypeStruct((BINS, 64,...  2.87 us

profile of v1, /device:TPU:1, one launch (start us, length us, event | category | flops | bytes accessed | tf_op | source)
XLA Modules:
  0.0 114.5 jit_solution(4421259719642815166)
XLA Ops:
  0.0 0.7 copy.10.keep
  0.7 0.0 copy-start.1
  0.7 1.2 %copy-done.1 = bf16[8,16,4352]{2,1,0:T(8,128)(2,1)S(1)} copy-done((bf16[8,16,4352]{2,1,0:T(8,128)(2,1)S(1)}, bf16[8,16,4352]{2,1,0:T(8,128)(2,1)}, u32[]{:S(2)}) %copy-start.1) | copy-done | bytes 1114136
  2.0 0.0 copy-start.2
  2.0 0.9 copy-done.2
  2.9 0.0 copy-start.3
  2.9 0.9 copy-done.3
  3.9 0.0 copy-start.4
  3.9 0.7 copy-done.4
  4.6 0.0 copy-start.5
  4.6 0.7 copy-done.5
  5.3 0.0 copy-start.6
  5.3 0.7 copy-done.6
  6.0 9.0 %transform.1.send = bf16[32,64,128]{2,1,0:T(8,128)(2,1)S(1)} custom-call(s32[8]{0:T(128)S(1)} %copy-done.6, bf16[8,16,4352]{2,1,0:T(8,128)(2,1)S(1)} %copy-done.1, s32[16,1]{1,0:T(8,128)S(1)} %copy.10.keep, f32[16,256]{1,0:T(8,128)S(1)} %copy-done.5, f32[16,256]{1,0:T(8,128)S(1)} %copy-done.4, bf16[512,256]{1,0:T(8,128)(2,1)S(1)} %copy-done.3, ...), custom_call_target="tpu_custom_call" | custom-call | tf_op jit(solution)/shard_map/transform/pallas_call | solution.py:165
  14.9 15.8 %to_bins.1.recv = bf16[32,64,128]{2,1,0:T(8,128)(2,1)S(1)} custom-call(bf16[32,64,128]{2,1,0:T(8,128)(2,1)S(1)} %transform.1.send), custom_call_target="tpu_custom_call" | custom-call | tf_op jit(solution)/shard_map/to_bins/pallas_call | solution.py:229
  30.8 2.9 %relayout.1.own = bf16[32,64,128]{2,1,0:T(8,128)(2,1)S(1)} custom-call(bf16[32,64,128]{2,1,0:T(8,128)(2,1)S(1)} %to_bins.1.recv), custom_call_target="tpu_custom_call" | custom-call | tf_op jit(solution)/shard_map/relayout/pallas_call | solution.py:310
  33.6 41.5 %halo.1 = bf16[2,32,64,128]{3,2,1,0:T(8,128)(2,1)S(1)} custom-call(bf16[32,64,128]{2,1,0:T(8,128)(2,1)S(1)} %relayout.1.own), custom_call_target="tpu_custom_call" | custom-call | tf_op jit(solution)/shard_map/halo/pallas_call | solution.py:272
  75.2 0.0 copy-start
  75.2 15.7 %cross.1.send = bf16[32,128,128]{2,1,0:T(8,128)(2,1)S(1)} custom-call(bf16[32,64,128]{2,1,0:T(8,128)(2,1)S(1)} %relayout.1.own, bf16[2,32,64,128]{3,2,1,0:T(8,128)(2,1)S(1)} %halo.1), custom_call_target="tpu_custom_call" | custom-call | tf_op jit(solution)/shard_map/cross/pallas_call | solution.py:359
  90.9 20.7 %to_offsets.1.spectra = bf16[32,128,128]{2,1,0:T(8,128)(2,1)S(1)} custom-call(bf16[32,128,128]{2,1,0:T(8,128)(2,1)S(1)} %cross.1.send), custom_call_target="tpu_custom_call" | custom-call | tf_op jit(solution)/shard_map/to_offsets/pallas_call | solution.py:229
  111.6 0.0 copy-done
  111.6 1.5 %lags.1 = f32[4,256,128]{2,1,0:T(8,128)S(1)} custom-call(bf16[32,128,128]{2,1,0:T(8,128)(2,1)S(1)} %to_offsets.1.spectra, bf16[2048,512]{1,0:T(8,128)(2,1)S(1)} %copy-done), custom_call_target="tpu_custom_call" | custom-call | tf_op jit(solution)/shard_map/lags/pallas_call | solution.py:384
  113.1 0.3 copy.11
  113.5 1.0 reshape.7
Async XLA Ops:
  0.7 1.2 %copy-start.1 = (bf16[8,16,4352]{2,1,0:T(8,128)(2,1)S(1)}, bf16[8,16,4352]{2,1,0:T(8,128)(2,1)}, u32[]{:S(2)}) copy-start(bf16[8,16,4352]{2,1,0:T(8,128)(2,1)} %raw.1) | copy-start | bytes 3342340
  2.0 0.9 copy-start.2
  2.9 0.9 copy-start.3
  3.9 0.7 copy-start.4
  4.6 0.7 copy-start.5
  5.3 0.7 copy-start.6
  75.2 36.4 %copy-start = (bf16[2048,512]{1,0:T(8,128)(2,1)S(1)}, bf16[2048,512]{1,0:T(8,128)(2,1)}, u32[]{:S(2)}) copy-start(bf16[2048,512]{1,0:T(8,128)(2,1)} %constant.14.clone.table) | copy-start | bytes 6291460

commit v2 on v0

v2 whole, which is shorter than its diff:
```python
import functools
import math

import jax
import jax.numpy as jnp
import numpy as np
from jax import lax
from jax.experimental import pallas as pl
from jax.experimental.pallas import tpu as pltpu
from jax.sharding import PartitionSpec as P

MESH = pl.DeviceIdType.MESH
L = 4096
BAND_LO = 64
NB = 1024
SMOOTH = 64
LAGS = 512
SPAN = 128
EPS = 1e-06
RADIX = 16
TAIL = L // RADIX
PLANE = 32
WIN = 8
QUAD = 4
BINS = 32
CHUNK = 8
REL_PITCH = 40
OUT_PITCH = 72
SLOTS = 8
GROUP = 4
F32 = jnp.float32
BF16 = jnp.bfloat16


def second_stage():
    b = np.arange(TAIL)[:, None]
    lane = np.arange(128)[None, :]
    half, imag, low = lane // 64, (lane // 32) % 2, lane % 32
    angle = 2.0 * np.pi * ((b * (BAND_LO // RADIX + half * 32 + low)) % TAIL) / TAIL
    cos, sin = np.cos(angle), np.sin(angle)
    real = np.concatenate([cos, sin], 0)
    imaginary = np.concatenate([-sin, cos], 0)
    straight = np.where(imag == 0, real, imaginary)
    turned = np.where(imag == 0, -imaginary, real)
    whole = np.concatenate([straight, turned], 1).astype(np.float32)
    high = whole.astype(jnp.bfloat16)
    low_part = (whole - high.astype(np.float32)).astype(jnp.bfloat16)
    return high, low_part


def twiddles():
    f = np.arange(RADIX)[:, None]
    b = np.arange(TAIL)[None, :]
    angle = 2.0 * np.pi * (f * b) / L
    return np.cos(angle).astype(np.float32), np.sin(angle).astype(np.float32)


def lag_rows():
    frequency = np.arange(NB, dtype=np.int64) + BAND_LO
    lag_index = np.arange(LAGS, dtype=np.int64) - LAGS // 2
    turns = np.mod(frequency[:, None] * lag_index[None, :], L).astype(np.float32)
    angles = turns * np.float32(2.0 * math.pi / L)
    cos, sin = np.cos(angles.astype(np.float64)), np.sin(angles.astype(np.float64))
    table = np.stack([cos, -sin], 1).astype(np.float32)
    bins = RADIX * np.arange(64)[None, :] + np.arange(RADIX)[:, None]
    return table[bins].reshape(2 * NB, LAGS).astype(jnp.bfloat16)


def real_fft(x):
    n = len(x)
    if n == 2:
        return [(x[0] + x[1], None), (x[0] - x[1], None)]
    even, odd = real_fft(x[0::2]), real_fft(x[1::2])
    half, quarter = n // 2, n // 4
    out = [None] * (half + 1)
    out[0] = (even[0][0] + odd[0][0], None)
    out[half] = (even[0][0] - odd[0][0], None)
    for k in range(1, quarter):
        (er, ei), (orr, oi) = even[k], odd[k]
        c, s = math.cos(2.0 * math.pi * k / n), math.sin(2.0 * math.pi * k / n)
        if 8 * k == n:
            tr, ti = (orr + oi) * c, (oi - orr) * c
        else:
            tr, ti = orr * c + oi * s, oi * c - orr * s
        out[k] = (er + tr, ei + ti)
        out[half - k] = (er - tr, ti - ei)
    out[quarter] = (even[quarter][0], -odd[quarter][0])
    return out


def place():
    fibre, win = lax.axis_index("fibre"), lax.axis_index("win")
    return fibre // QUAD, win * QUAD + fibre % QUAD


def device(z, s):
    return (z * QUAD + s % QUAD, s // QUAD)


def greet_all(planes, z, me):
    barrier = pltpu.get_barrier_semaphore()

    def signal(plane, s):
        pl.semaphore_signal(barrier, inc=1, device_id=device(plane, s), device_id_type=MESH)

    def near(j, carry):
        signal(z, (me + j) % PLANE)
        return carry

    def far(j, carry):
        signal((z + 1) % planes, (me + j) % PLANE)
        return carry

    lax.fori_loop(1, PLANE, near, 0)
    signal((z + 1) % planes, me)
    signal((z + planes - 1) % planes, me)

    @pl.when(me % QUAD + me // QUAD >= WIN - 1)
    def _():
        lax.fori_loop(0, PLANE, far, 0)

    return PLANE - 1 + 2 + 10


def first_stage(offsets, raw, tw_cos, tw_sin, lhs, phase_cos, phase_sin):
    width = 128

    def one_window(w, carry):
        off = offsets[w]
        u = lax.broadcasted_iota(jnp.int32, (RADIX, TAIL), 0) * TAIL + lax.broadcasted_iota(
            jnp.int32, (RADIX, TAIL), 1
        )
        taper = 0.5 - 0.5 * jnp.cos(((u - off) & (L - 1)).astype(F32) * (2.0 * math.pi / L))
        f = lax.broadcasted_iota(jnp.int32, (RADIX, 128), 0)
        lane = lax.broadcasted_iota(jnp.int32, (RADIX, 128), 1)
        k = (BAND_LO // RADIX + (lane // 64) * 32 + lane % 32) * RADIX + f
        angle = ((k * off) & (L - 1)).astype(F32) * (2.0 * math.pi / L)
        phase_cos[w] = jnp.cos(angle)
        phase_sin[w] = jnp.sin(angle)

        def tiles_of(low, size):
            wrapped = lax.broadcasted_iota(jnp.int32, (16, size), 1) + low < off
            first = jnp.where(
                wrapped, raw[w, :, L + low : L + low + size].astype(F32), raw[w, :, low : low + size].astype(F32)
            )
            return [first] + [
                raw[w, :, a * TAIL + low : a * TAIL + low + size].astype(F32) for a in range(1, RADIX)
            ]

        total = functools.reduce(lambda p, q: p + q, tiles_of(0, TAIL))
        mean = jnp.sum(total, axis=1, keepdims=True) * (1.0 / L)
        rows = pl.ds(pl.multiple_of(w * 16, 16), 16)
        for low in range(0, TAIL, width):
            span = slice(low, low + width)
            spectrum = real_fft([(x - mean) * taper[a : a + 1, span] for a, x in enumerate(tiles_of(low, width))])
            for f in range(RADIX):
                re, im = spectrum[f] if f <= RADIX // 2 else spectrum[RADIX - f]
                if f > RADIX // 2:
                    im = -im
                if f:
                    c, s = tw_cos[f : f + 1, span], tw_sin[f : f + 1, span]
                    re, im = (re * c, -re * s) if im is None else (re * c + im * s, im * c - re * s)
                else:
                    im = jnp.zeros_like(re)
                for part, value in enumerate((re, im)):
                    high = value.astype(BF16)
                    start = part * TAIL + low
                    lhs[f, rows, start : start + width] = high
                    start += 2 * TAIL
                    lhs[f, rows, start : start + width] = (value - high.astype(F32)).astype(BF16)
        return carry

    lax.fori_loop(0, 8, one_window, 0)


def second_stage_of(lhs, w_hi, w_lo, kept, phase_cos, phase_sin):
    def some_columns(index, power):
        start = index * GROUP
        whole = lhs[pl.ds(start, GROUP)].reshape(GROUP * 128, 4 * TAIL)
        high, low = whole[:, : 2 * TAIL], whole[:, 2 * TAIL :]
        both = (
            jnp.dot(high, w_hi[...], preferred_element_type=F32)
            + jnp.dot(high, w_lo[...], preferred_element_type=F32)
            + jnp.dot(low, w_hi[...], preferred_element_type=F32)
        )
        for j in range(GROUP):
            c = phase_cos[:, pl.ds(start + j, 1), :]
            s = phase_sin[:, pl.ds(start + j, 1), :]
            one = both[j * 128 : (j + 1) * 128].reshape(8, 16, 256)
            value = (one[:, :, :128] * c + one[:, :, 128:] * s).reshape(128, 128)
            kept[start + j] = value
            power = power + value * value
        return power

    return lax.fori_loop(0, RADIX // GROUP, some_columns, jnp.zeros((128, 128), F32))


def whitening(power, mask):
    row = lax.broadcasted_iota(jnp.int32, (128, 128), 0)
    col = lax.broadcasted_iota(jnp.int32, (128, 128), 1)
    same = (row // 64 == col // 64) & ((row % 32) // 4 == (col % 32) // 4)
    block = jnp.where(same, 1.0, 0.0).astype(F32)
    mean_power = jnp.dot(power, block, precision=lax.Precision.HIGHEST, preferred_element_type=F32) * (1.0 / SMOOTH)
    channel = lax.broadcasted_iota(jnp.int32, (16, 128), 0)
    flag = jnp.zeros((16, 128), F32)
    for c in range(16):
        flag = jnp.where(channel == c, mask[c].astype(F32), flag)
    flag = jnp.broadcast_to(flag[None], (8, 16, 128)).reshape(128, 128)
    return (1.0 / jnp.sqrt(mean_power + EPS)) * flag


def main_kernel(
    planes, offsets, mask, raw_hbm, cos_hbm, sin_hbm, hi_hbm, lo_hbm, got_near, got_far,
    raw, tw_cos, tw_sin, w_hi, w_lo, lhs, kept, phase_cos, phase_sin,
    send, recv, turned, own, halo, near, far, near_col, far_col, send_near, send_far,
    in_sem, own_sem, s_send, s_recv, h_send, h_recv, x_send, x_recv,
):
    z, me = place()
    my_q, my_v = me % QUAD, me // QUAD
    loads = [
        pltpu.make_async_copy(source, target, in_sem.at[i])
        for i, (source, target) in enumerate(
            ((raw_hbm, raw), (cos_hbm, tw_cos), (sin_hbm, tw_sin), (hi_hbm, w_hi), (lo_hbm, w_lo))
        )
    ]
    for load in loads:
        load.start()
    expected = greet_all(planes, z, me)
    for slot in range(SLOTS):
        near_col[slot, 128:, :] = jnp.zeros((128, 128), F32)
        far_col[slot, :128, :] = jnp.zeros((128, 128), F32)
    for load in loads[:3]:
        load.wait()

    first_stage(offsets, raw, tw_cos, tw_sin, lhs, phase_cos, phase_sin)
    for load in loads[3:]:
        load.wait()
    factor = whitening(second_stage_of(lhs, w_hi, w_lo, kept, phase_cos, phase_sin), mask)
    left = lax.broadcasted_iota(jnp.int32, (64, 128), 1) < 64
    pl.semaphore_wait(pltpu.get_barrier_semaphore(), expected)

    def bins_copy(to):
        return pltpu.make_async_remote_copy(
            src_ref=send.at[to],
            dst_ref=recv.at[me],
            send_sem=s_send.at[to],
            recv_sem=s_recv.at[me],
            device_id=device(z, to),
            device_id_type=MESH,
        )

    def bins_wait(source):
        return pltpu.make_async_remote_copy(
            src_ref=send.at[source],
            dst_ref=recv.at[source],
            send_sem=s_send.at[source],
            recv_sem=s_recv.at[source],
            device_id=device(z, source),
            device_id_type=MESH,
        )

    kept_here = pltpu.make_async_copy(send.at[me], recv.at[me], own_sem.at[0])

    def launch(to):
        @pl.when(to != me)
        def _():
            bins_copy(to).start()

        @pl.when(to == me)
        def _():
            kept_here.start()

    def one_store(j, carry):
        f = (me // 2 + j) % RADIX
        value = kept[f] * factor
        top, bottom = value[:64], value[64:]
        send[2 * f] = jnp.where(left, top, pltpu.roll(bottom, 64, 1)).astype(BF16)
        send[2 * f + 1] = jnp.where(left, pltpu.roll(top, 64, 1), bottom).astype(BF16)
        launch(2 * f)
        launch(2 * f + 1)
        return carry

    lax.fori_loop(0, RADIX, one_store, 0)
    kept_here.wait()

    def one_block(j, carry):
        v = (my_v + j) % WIN
        for q in range(QUAD):
            source = v * QUAD + q

            @pl.when(source != me)
            def _():
                bins_wait(source).wait_recv()

        for w in range(2):
            parts = [
                recv[v * QUAD + q, (p * 2 + w) * 16 : (p * 2 + w + 1) * 16, :] for p in range(2) for q in range(QUAD)
            ]
            block = jnp.concatenate([part.astype(F32) for part in parts], 0).T
            for h in range(4):
                start = pl.multiple_of(((v * 2 + w) * 4 + h) * REL_PITCH, 8)
                turned[pl.ds(start, 32), :] = block[h * 32 : (h + 1) * 32]
        return carry

    lax.fori_loop(0, WIN, one_block, 0)

    def halo_copy(way, chunk):
        span = pl.ds(chunk * CHUNK, CHUNK)
        return pltpu.make_async_remote_copy(
            src_ref=own.at[span],
            dst_ref=halo.at[way, span],
            send_sem=h_send.at[way, chunk],
            recv_sem=h_recv.at[way, chunk],
            device_id=device((z + (planes - 1 if way == 0 else 1)) % planes, me),
            device_id_type=MESH,
        )

    def gather(chunk, carry):
        for j in range(CHUNK):
            g = chunk * CHUNK + j
            real = turned[pl.ds(g, 32, stride=2 * REL_PITCH), :]
            imag = turned[pl.ds(REL_PITCH + g, 32, stride=2 * REL_PITCH), :]
            own[g] = jnp.concatenate([real, imag], 0).astype(BF16)
        halo_copy(0, chunk).start()
        halo_copy(1, chunk).start()
        return carry

    lax.fori_loop(0, BINS // CHUNK, gather, 0)

    def operand(x, rx):
        y = jnp.concatenate([x[32:], -x[:32]], 0)
        ry = jnp.concatenate([rx[32:], -rx[:32]], 0)
        return jnp.concatenate([jnp.where(left, x, ry), jnp.where(left, rx, y)], 0).T.astype(BF16)

    def cross(chunk, carry):
        halo_copy(0, chunk).wait_recv()
        halo_copy(1, chunk).wait_recv()
        for j in range(CHUNK):
            g = chunk * CHUNK + j
            a = own[g].astype(F32)
            e = jnp.where(z + 1 < planes, halo[0, g].astype(F32), 0.0)
            m = jnp.where(z > 0, halo[1, g].astype(F32), 0.0)
            ra, re, rm = (pltpu.roll(x, 64, 1) for x in (a, e, m))
            right = jnp.concatenate([jnp.where(left, a, re), jnp.where(left, ra, e)], 0).astype(BF16)
            last = jnp.concatenate([e, re], 0).astype(BF16)
            for ref, value in (
                (near, jnp.dot(operand(a, ra), right, preferred_element_type=F32)),
                (far, jnp.dot(operand(m, rm), last, preferred_element_type=F32)),
            ):
                for part in range(2):
                    start = pl.multiple_of((g * 2 + part) * OUT_PITCH, 8)
                    ref[pl.ds(start, 64), :] = value[part * 64 : (part + 1) * 64]
        return carry

    lax.fori_loop(0, BINS // CHUNK, cross, 0)

    def offsets_copy(kind, to):
        return pltpu.make_async_remote_copy(
            src_ref=(send_near, send_far)[kind].at[to],
            dst_ref=(got_near, got_far)[kind].at[me],
            send_sem=x_send.at[kind, to],
            recv_sem=x_recv.at[kind, me],
            device_id=device(z if kind == 0 else (z + planes - 1) % planes, to),
            device_id_type=MESH,
        )

    def offsets_wait(kind, source):
        return pltpu.make_async_remote_copy(
            src_ref=(send_near, send_far)[kind].at[source],
            dst_ref=(got_near, got_far)[kind].at[source],
            send_sem=x_send.at[kind, source],
            recv_sem=x_recv.at[kind, source],
            device_id=device(z if kind == 0 else (z + 1) % planes, source),
            device_id_type=MESH,
        )

    kept_near = pltpu.make_async_copy(send_near.at[me], got_near.at[me], own_sem.at[1])
    wide = lax.broadcasted_iota(jnp.int32, (128, 128), 1) < 64

    def one_quarter(j, carry):
        q = (my_q + j) % QUAD

        def one_pair(i, carry):
            c = q * 16 + i
            slot = i
            for ref, column, base, size, target in (
                (near, near_col, 0, 128, send_near), (far, far_col, 128, 64, send_far)
            ):
                block = jnp.concatenate(
                    [ref[pl.ds(c, 64, stride=OUT_PITCH), :], ref[pl.ds(c + 8, 64, stride=OUT_PITCH), :]], 0
                )
                column[slot, base : base + size, :] = block.T[:size]
                value = jnp.where(
                    wide, column[slot, pl.ds(c + 1, 128), :], column[slot, pl.ds(c + 9, 128), :]
                ).astype(BF16)
                rows = pl.ds(pl.multiple_of(i * 16, 16), 16)
                for v in range(WIN):
                    target[v * QUAD + q, rows, :] = value[v * 16 : (v + 1) * 16]
            return carry

        lax.fori_loop(0, 8, one_pair, 0, unroll=4)

        def one_send(k, carry):
            v = (my_v + k) % WIN
            to = v * QUAD + q

            @pl.when((v + q < WIN) & (to != me))
            def _():
                offsets_copy(0, to).start()

            @pl.when((v + q < WIN) & (to == me))
            def _():
                kept_near.start()

            @pl.when(v + q >= WIN - 1)
            def _():
                offsets_copy(1, to).start()

            return carry

        lax.fori_loop(0, WIN, one_send, 0)
        return carry

    lax.fori_loop(0, QUAD, one_quarter, 0)

    @pl.when(my_v + my_q < WIN)
    def _():
        def one(j, carry):
            offsets_wait(0, (me + j) % PLANE).wait_recv()
            return carry

        lax.fori_loop(1, PLANE, one, 0)
        kept_near.wait()

    @pl.when(my_v + my_q >= WIN - 1)
    def _():
        def one(source, carry):
            offsets_wait(1, source).wait_recv()
            return carry

        lax.fori_loop(0, PLANE, one, 0)

    def drain(to, carry):
        q, v = to % QUAD, to // QUAD

        @pl.when(to != me)
        def _():
            bins_copy(to).wait_send()

        @pl.when((v + q < WIN) & (to != me))
        def _():
            offsets_copy(0, to).wait_send()

        @pl.when(v + q >= WIN - 1)
        def _():
            offsets_copy(1, to).wait_send()

        return carry

    lax.fori_loop(0, PLANE, drain, 0)

    def drain_halo(chunk, carry):
        halo_copy(0, chunk).wait_send()
        halo_copy(1, chunk).wait_send()
        return carry

    lax.fori_loop(0, BINS // CHUNK, drain_halo, 0)


def cross_spectra(raw, offsets, mask, planes):
    w_hi, w_lo = (jnp.asarray(x) for x in second_stage())
    tw_cos, tw_sin = (jnp.asarray(x) for x in twiddles())
    vmem = pl.BlockSpec(memory_space=pltpu.VMEM)
    smem = pl.BlockSpec(memory_space=pltpu.SMEM)
    anywhere = pl.BlockSpec(memory_space=pltpu.HBM)
    packet = jax.ShapeDtypeStruct((PLANE, 128, 128), BF16)
    dma = pltpu.SemaphoreType.DMA
    return pl.pallas_call(
        functools.partial(main_kernel, planes),
        out_shape=[packet, packet],
        in_specs=[smem, smem] + [anywhere] * 5,
        out_specs=[vmem, vmem],
        scratch_shapes=[
            pltpu.VMEM(raw.shape, BF16),
            pltpu.VMEM(tw_cos.shape, F32),
            pltpu.VMEM(tw_sin.shape, F32),
            pltpu.VMEM(w_hi.shape, BF16),
            pltpu.VMEM(w_lo.shape, BF16),
            pltpu.VMEM((RADIX, 128, 4 * TAIL), BF16),
            pltpu.VMEM((RADIX, 128, 128), F32),
            pltpu.VMEM((8, RADIX, 128), F32),
            pltpu.VMEM((8, RADIX, 128), F32),
            pltpu.VMEM((PLANE, 64, 128), BF16),
            pltpu.VMEM((PLANE, 64, 128), BF16),
            pltpu.VMEM((64 * REL_PITCH, 128), F32),
            pltpu.VMEM((BINS, 64, 128), BF16),
            pltpu.VMEM((2, BINS, 64, 128), BF16),
            pltpu.VMEM((2 * BINS * OUT_PITCH, 128), F32),
            pltpu.VMEM((2 * BINS * OUT_PITCH, 128), F32),
            pltpu.VMEM((SLOTS, 256, 128), F32),
            pltpu.VMEM((SLOTS, 256, 128), F32),
            pltpu.VMEM((PLANE, 128, 128), BF16),
            pltpu.VMEM((PLANE, 128, 128), BF16),
            dma((5,)),
            dma((2,)),
            dma((PLANE,)),
            dma((PLANE,)),
            dma((2, BINS // CHUNK)),
            dma((2, BINS // CHUNK)),
            dma((2, PLANE)),
            dma((2, PLANE)),
        ],
        compiler_params=pltpu.CompilerParams(
            collective_id=0, has_side_effects=True, vmem_limit_bytes=40 * 2**20
        ),
        name="main",
    )(*(pltpu.with_memory_space_constraint(x, pltpu.HBM) for x in (offsets, mask, raw, tw_cos, tw_sin, w_hi, w_lo)))


def lag_kernel(scale, near, far, table, out, lhs):
    _, me = place()
    reach = me % QUAD + me // QUAD
    left = lax.broadcasted_iota(jnp.int32, (128, 128), 1) < 64

    def packet(s):
        return jnp.where(reach < WIN, near[s].astype(F32), 0.0) + jnp.where(
            reach >= WIN - 1, far[s].astype(F32), 0.0
        )

    for f in range(RADIX):
        one, two = packet(2 * f), packet(2 * f + 1)
        lhs[:128, f * 128 : (f + 1) * 128] = jnp.where(left, one, pltpu.roll(two, 64, 1)).astype(BF16)
        lhs[128:, f * 128 : (f + 1) * 128] = jnp.where(left, pltpu.roll(one, 64, 1), two).astype(BF16)
    for part in range(LAGS // 128):
        span = slice(part * 128, (part + 1) * 128)
        lags = jnp.dot(lhs[...], table[:, span], preferred_element_type=F32) * scale
        for c in range(16):
            out[:, c, span] = lags[c * 16 : (c + 1) * 16]


def lag_transform(near, far, scale):
    vmem = pl.BlockSpec(memory_space=pltpu.VMEM)
    return pl.pallas_call(
        functools.partial(lag_kernel, scale),
        out_shape=jax.ShapeDtypeStruct((16, 16, LAGS), F32),
        in_specs=[vmem, vmem, vmem],
        out_specs=vmem,
        scratch_shapes=[pltpu.VMEM((256, 2 * NB), BF16)],
        compiler_params=pltpu.CompilerParams(vmem_limit_bytes=24 * 2**20),
        name="lags",
    )(near, far, lag_rows())


def body(planes, raw, offsets, mask):
    near, far = cross_spectra(raw, offsets, mask, planes)
    return lag_transform(near, far, 1.0 / math.sqrt(NB * 8 * WIN))


def solution(mesh):
    planes = mesh.shape["fibre"] // QUAD
    return jax.shard_map(
        functools.partial(body, planes),
        mesh=mesh,
        in_specs=(P("win", "fibre", None), P("win"), P("fibre")),
        out_specs=P("win", "fibre", None),
        check_vma=False,
    )
```

time: 447 us -> 65.7 us (0.15)
  waiting for transfers between devices: 190 us -> 0 us
  local copies, waits for them, and re-layouts: 104 us -> 1.59 us
  other arithmetic: 90.8 us -> 0 us
  Pallas kernels: 0 us -> 63.9 us
  matrix products: 28.2 us -> 0 us
  starting transfers between devices: 14.1 us -> 0 us
  between operations: 13.7 us -> 0.02 us
  loops' own time: 5.67 us -> 0 us
    ppermute x8 -> x0, waiting for transfers between devices: 96.1 us -> none  [from_behind(): return lax.ppermute(array, axis, pairs)]
    reduce_scatter x1 -> x0, waiting for transfers between devices: 93.7 us -> none  [body(): lax.psum_scatter(results.reshape(block_rows * lax.axis_size('win'), chann...]
    reduce_sum x9 -> x0, other arithmetic: 72.6 us -> none  [the longest x8 72.4 us: correlate(): cross_real = jnp.sum(own_real * other_real + own_imag * other_imag, axis=1)]
    pallas_call x0 -> x2, Pallas kernels: none -> 63.9 us  [the longest x1 61.3 us: cross_spectra(): pl.pallas_call(functools.partial(main_kernel, planes), out_shape=[packet,...]
    gather x32 -> x0, local copies, waits for them, and re-layouts: 62.4 us -> none  [the longest x8 39 us: partner_block(): lax.dynamic_slice_in_dim(segment, first, channels, 1)]
    dot_general x14 -> x0, matrix products: 28.2 us -> none  [the longest x8 12.2 us: correlate(): jnp.dot(cross.reshape(count * channels, 2 * half), table, preferred_eleme...]
    dynamic_slice x16 -> x0, local copies, waits for them, and re-layouts: 15.1 us -> none  [the longest x8 10.3 us: one_group(): lax.dynamic_slice_in_dim(extended, first + 1, channels + block_rows - 1, 1)]
    ppermute x8 -> x0, starting transfers between devices: 14.1 us -> none  [from_behind(): return lax.ppermute(array, axis, pairs)]
  transfers between devices with their start and end apart: 9 -> 0, of which waited for: 7 -> 0; matrix products, arithmetic and copies ran while one was open for 4% -> 0% of each run, Pallas kernels for 0% -> 0%
where the time goes in v2:
time: 65.7 us; the launch traced here: 65.5 us
  Pallas kernels  63.9 us (97%)
  local copies, waits for them, and re-layouts  1.59 us (2%)
    pallas_call x1, Pallas kernels, cross_spectra(): pl.pallas_call(functools.partial(main_kernel, planes), out_shape=[packet,...  61.3 us
    pallas_call x1, Pallas kernels, lag_transform(): pl.pallas_call(functools.partial(lag_kernel, scale), out_shape=jax.ShapeD...  2.65 us
    unnamed x2, local copies, waits for them, and re-layouts  1.59 us

profile of v2, /device:TPU:1, one launch (start us, length us, event | category | flops | bytes accessed | tf_op | source)
XLA Modules:
  0.0 65.5 jit_solution(6948498430438213302)
XLA Ops:
  0.0 61.3 %main.1 = (bf16[32,128,128]{2,1,0:T(8,128)(2,1)S(1)}, bf16[32,128,128]{2,1,0:T(8,128)(2,1)S(1)}) custom-call(s32[8]{0:T(128)} %offsets.1, s32[16]{0:T(128)} %mask.1, bf16[8,16,4352]{2,1,0:T(8,128)(2,1)} %raw_hbm.1, f32[16,256]{1,0:T(8,128)} %constant.12.clone.cos_hbm, f32[16,256]{1,0:T(8,128)} %constant.13.clone.sin_hbm, ...), custom_call_target="tpu_custom_call" | custom-call | tf_op jit(solution)/shard_map/main/pallas_call | solution.py:478
  61.3 0.0 copy-start
  61.3 1.6 %copy-done = bf16[2048,512]{1,0:T(8,128)(2,1)S(1)} copy-done((bf16[2048,512]{1,0:T(8,128)(2,1)S(1)}, bf16[2048,512]{1,0:T(8,128)(2,1)}, u32[]{:S(2)}) %copy-start) | copy-done | bytes 2097176
  62.9 2.6 %lags.1 = f32[16,16,512]{2,1,0:T(8,128)} custom-call(bf16[32,128,128]{2,1,0:T(8,128)(2,1)S(1)} %get-tuple-element.7.near, bf16[32,128,128]{2,1,0:T(8,128)(2,1)S(1)} %get-tuple-element.8.far, bf16[2048,512]{1,0:T(8,128)(2,1)S(1)} %copy-done), custom_call_target="tpu_custom_call" | custom-call | tf_op jit(solution)/shard_map/lags/pallas_call | solution.py:543
Async XLA Ops:
  61.3 1.6 %copy-start = (bf16[2048,512]{1,0:T(8,128)(2,1)S(1)}, bf16[2048,512]{1,0:T(8,128)(2,1)}, u32[]{:S(2)}) copy-start(bf16[2048,512]{1,0:T(8,128)(2,1)} %constant.14.clone.table) | copy-start | bytes 6291460

commit v3 on v2

v3 whole, which is shorter than its diff:
```python
import functools
import math

import jax
import jax.numpy as jnp
import numpy as np
from jax import lax
from jax.experimental import pallas as pl
from jax.experimental.pallas import tpu as pltpu
from jax.sharding import PartitionSpec as P

MESH = pl.DeviceIdType.MESH
L = 4096
BAND_LO = 64
NB = 1024
SMOOTH = 64
LAGS = 512
SPAN = 128
EPS = 1e-06
RADIX = 16
TAIL = L // RADIX
PLANE = 32
WIN = 8
QUAD = 4
BINS = 32
CHUNK = 8
REL_PITCH = 40
OUT_PITCH = 72
SLOTS = 8
HALVES = 2
ROWS = 128 // HALVES
CHUNKS = BINS // CHUNK
GROUP = 8
F32 = jnp.float32
BF16 = jnp.bfloat16


def second_stage():
    b = np.arange(TAIL)[:, None]
    lane = np.arange(128)[None, :]
    half, imag, low = lane // 64, (lane // 32) % 2, lane % 32
    angle = 2.0 * np.pi * ((b * (BAND_LO // RADIX + half * 32 + low)) % TAIL) / TAIL
    cos, sin = np.cos(angle), np.sin(angle)
    real = np.concatenate([cos, sin], 0)
    imaginary = np.concatenate([-sin, cos], 0)
    straight = np.where(imag == 0, real, imaginary)
    turned = np.where(imag == 0, -imaginary, real)
    whole = np.concatenate([straight, turned], 1).astype(np.float32)
    high = whole.astype(jnp.bfloat16)
    low_part = (whole - high.astype(np.float32)).astype(jnp.bfloat16)
    return high, low_part


def twiddles():
    f = np.arange(RADIX)[:, None]
    b = np.arange(TAIL)[None, :]
    angle = 2.0 * np.pi * (f * b) / L
    return np.cos(angle).astype(np.float32), np.sin(angle).astype(np.float32)


def lag_rows():
    frequency = np.arange(NB, dtype=np.int64) + BAND_LO
    lag_index = np.arange(LAGS, dtype=np.int64) - LAGS // 2
    turns = np.mod(frequency[:, None] * lag_index[None, :], L).astype(np.float32)
    angles = turns * np.float32(2.0 * math.pi / L)
    cos, sin = np.cos(angles.astype(np.float64)), np.sin(angles.astype(np.float64))
    table = np.stack([cos, -sin], 1).astype(np.float32)
    bins = RADIX * np.arange(64)[None, :] + np.arange(RADIX)[:, None]
    return table[bins].reshape(2 * NB, LAGS).astype(jnp.bfloat16)


def real_fft(x):
    n = len(x)
    if n == 2:
        return [(x[0] + x[1], None), (x[0] - x[1], None)]
    even, odd = real_fft(x[0::2]), real_fft(x[1::2])
    half, quarter = n // 2, n // 4
    out = [None] * (half + 1)
    out[0] = (even[0][0] + odd[0][0], None)
    out[half] = (even[0][0] - odd[0][0], None)
    for k in range(1, quarter):
        (er, ei), (orr, oi) = even[k], odd[k]
        c, s = math.cos(2.0 * math.pi * k / n), math.sin(2.0 * math.pi * k / n)
        if 8 * k == n:
            tr, ti = (orr + oi) * c, (oi - orr) * c
        else:
            tr, ti = orr * c + oi * s, oi * c - orr * s
        out[k] = (er + tr, ei + ti)
        out[half - k] = (er - tr, ti - ei)
    out[quarter] = (even[quarter][0], -odd[quarter][0])
    return out


def place():
    fibre, win = lax.axis_index("fibre"), lax.axis_index("win")
    return fibre // QUAD, win * QUAD + fibre % QUAD


def device(z, s):
    return (z * QUAD + s % QUAD, s // QUAD)


def greet_all(planes, z, me):
    barrier = pltpu.get_barrier_semaphore()

    def signal(plane, s):
        pl.semaphore_signal(barrier, inc=1, device_id=device(plane, s), device_id_type=MESH)

    def near(j, carry):
        signal(z, (me + j) % PLANE)
        return carry

    lax.fori_loop(1, PLANE, near, 0)
    signal((z + 1) % planes, me)
    signal((z + planes - 1) % planes, me)
    return PLANE - 1 + 2


def first_stage(half, offsets, raw, tw_cos, tw_sin, lhs, phase_cos, phase_sin):
    width = 128

    def one_window(i, carry):
        w = (i // 2) * 4 + half * 2 + i % 2
        off = offsets[w]
        u = lax.broadcasted_iota(jnp.int32, (RADIX, TAIL), 0) * TAIL + lax.broadcasted_iota(
            jnp.int32, (RADIX, TAIL), 1
        )
        taper = 0.5 - 0.5 * jnp.cos(((u - off) & (L - 1)).astype(F32) * (2.0 * math.pi / L))
        f = lax.broadcasted_iota(jnp.int32, (RADIX, 128), 0)
        lane = lax.broadcasted_iota(jnp.int32, (RADIX, 128), 1)
        k = (BAND_LO // RADIX + (lane // 64) * 32 + lane % 32) * RADIX + f
        angle = ((k * off) & (L - 1)).astype(F32) * (2.0 * math.pi / L)
        phase_cos[i] = jnp.cos(angle)
        phase_sin[i] = jnp.sin(angle)

        def tiles_of(low, size):
            wrapped = lax.broadcasted_iota(jnp.int32, (16, size), 1) + low < off
            first = jnp.where(
                wrapped, raw[w, :, L + low : L + low + size].astype(F32), raw[w, :, low : low + size].astype(F32)
            )
            return [first] + [
                raw[w, :, a * TAIL + low : a * TAIL + low + size].astype(F32) for a in range(1, RADIX)
            ]

        total = functools.reduce(lambda p, q: p + q, tiles_of(0, TAIL))
        mean = jnp.sum(total, axis=1, keepdims=True) * (1.0 / L)
        rows = pl.ds(pl.multiple_of(i * 16, 16), 16)
        for low in range(0, TAIL, width):
            span = slice(low, low + width)
            spectrum = real_fft([(x - mean) * taper[a : a + 1, span] for a, x in enumerate(tiles_of(low, width))])
            for f in range(RADIX):
                re, im = spectrum[f] if f <= RADIX // 2 else spectrum[RADIX - f]
                if f > RADIX // 2:
                    im = -im
                if f:
                    c, s = tw_cos[f : f + 1, span], tw_sin[f : f + 1, span]
                    re, im = (re * c, -re * s) if im is None else (re * c + im * s, im * c - re * s)
                else:
                    im = jnp.zeros_like(re)
                for part, value in enumerate((re, im)):
                    high = value.astype(BF16)
                    start = part * TAIL + low
                    lhs[f, rows, start : start + width] = high
                    start += 2 * TAIL
                    lhs[f, rows, start : start + width] = (value - high.astype(F32)).astype(BF16)
        return carry

    lax.fori_loop(0, ROWS // 16, one_window, 0)


def second_stage_of(lhs, w_hi, w_lo, kept, phase_cos, phase_sin):
    def some_columns(index, power):
        start = index * GROUP
        whole = lhs[pl.ds(start, GROUP)].reshape(GROUP * ROWS, 4 * TAIL)
        both = jnp.dot(whole, w_hi[...], preferred_element_type=F32) + jnp.dot(
            whole[:, : 2 * TAIL], w_lo[...], preferred_element_type=F32
        )
        for j in range(GROUP):
            c = phase_cos[:, pl.ds(start + j, 1), :]
            s = phase_sin[:, pl.ds(start + j, 1), :]
            one = both[j * ROWS : (j + 1) * ROWS].reshape(ROWS // 16, 16, 256)
            value = (one[:, :, :128] * c + one[:, :, 128:] * s).reshape(ROWS, 128)
            kept[start + j] = value
            power = power + value * value
        return power

    return lax.fori_loop(0, RADIX // GROUP, some_columns, jnp.zeros((ROWS, 128), F32))


def whitening(power, mask):
    row = lax.broadcasted_iota(jnp.int32, (128, 128), 0)
    col = lax.broadcasted_iota(jnp.int32, (128, 128), 1)
    same = (row // 64 == col // 64) & ((row % 32) // 4 == (col % 32) // 4)
    block = jnp.where(same, 1.0, 0.0).astype(F32)
    mean_power = jnp.dot(power, block, precision=lax.Precision.HIGHEST, preferred_element_type=F32) * (1.0 / SMOOTH)
    channel = lax.broadcasted_iota(jnp.int32, (16, 128), 0)
    flag = jnp.zeros((16, 128), F32)
    for c in range(16):
        flag = jnp.where(channel == c, mask[c].astype(F32), flag)
    flag = jnp.broadcast_to(flag[None], (ROWS // 16, 16, 128)).reshape(ROWS, 128)
    return (1.0 / jnp.sqrt(mean_power + EPS)) * flag


def main_kernel(
    planes, scale, offsets, mask, raw_hbm, cos_hbm, sin_hbm, hi_hbm, lo_hbm, table_hbm, out,
    raw, tw_cos, tw_sin, w_hi, w_lo, table, lhs, kept, phase_cos, phase_sin,
    send, recv, turned, own, halo, near, far, near_col, far_col, send_near, send_far, got_far, got, lag_lhs,
    in_sem, own_sem, s_send, s_recv, h_send, h_recv, x_send, x_recv, f_send, f_recv,
):
    z, me = place()
    my_q, my_v = me % QUAD, me // QUAD
    above, below = (z + 1) % planes, (z + planes - 1) % planes
    loads = [
        pltpu.make_async_copy(source, target, in_sem.at[i])
        for i, (source, target) in enumerate(
            (
                (raw_hbm, raw),
                (cos_hbm, tw_cos),
                (sin_hbm, tw_sin),
                (hi_hbm, w_hi),
                (lo_hbm, w_lo),
                (table_hbm, table),
            )
        )
    ]
    for load in loads:
        load.start()
    expected = greet_all(planes, z, me)
    for slot in range(SLOTS):
        near_col[slot, 128:, :] = jnp.zeros((128, 128), F32)
        far_col[slot, :128, :] = jnp.zeros((128, 128), F32)
    for load in loads[:3]:
        load.wait()
    left = lax.broadcasted_iota(jnp.int32, (64, 128), 1) < 64

    def bins_copy(half, to, source):
        return pltpu.make_async_remote_copy(
            src_ref=send.at[half, to],
            dst_ref=recv.at[half, source],
            send_sem=s_send.at[half, to],
            recv_sem=s_recv.at[half, source],
            device_id=device(z, to),
            device_id_type=MESH,
        )

    def own_copy(half):
        return pltpu.make_async_copy(send.at[half, me], recv.at[half, me], own_sem.at[half])

    for half in range(HALVES):
        first_stage(half, offsets, raw, tw_cos, tw_sin, lhs, phase_cos, phase_sin)
        if half == 0:
            for load in loads[3:5]:
                load.wait()
        factor = whitening(second_stage_of(lhs, w_hi, w_lo, kept, phase_cos, phase_sin), mask)
        if half == 0:
            pl.semaphore_wait(pltpu.get_barrier_semaphore(), expected)

        def launch(to, half=half):
            @pl.when(to != me)
            def _():
                bins_copy(half, to, me).start()

            @pl.when(to == me)
            def _():
                own_copy(half).start()

        def one_store(j, carry, half=half, factor=factor, launch=launch):
            for k in range(2):
                f = (me // 2 + 2 * j + k) % RADIX
                value = kept[f] * factor
                top, bottom = value[:32], value[32:]
                send[half, 2 * f] = jnp.where(left[:32], top, pltpu.roll(bottom, 64, 1)).astype(BF16)
                send[half, 2 * f + 1] = jnp.where(left[:32], pltpu.roll(top, 64, 1), bottom).astype(BF16)
                launch(2 * f)
                launch(2 * f + 1)
            return carry

        lax.fori_loop(0, RADIX // 2, one_store, 0)

    def halo_copy(way, half, chunk):
        span = pl.ds(chunk * CHUNK, CHUNK)
        return pltpu.make_async_remote_copy(
            src_ref=own.at[half, span],
            dst_ref=halo.at[way, half, span],
            send_sem=h_send.at[way, half, chunk],
            recv_sem=h_recv.at[way, half, chunk],
            device_id=device(below if way == 0 else above, me),
            device_id_type=MESH,
        )

    for half in range(HALVES):
        own_copy(half).wait()

        def one_block(j, carry, half=half):
            v = (my_v + j) % WIN
            for q in range(QUAD):
                source = v * QUAD + q

                @pl.when(source != me)
                def _():
                    bins_copy(half, source, source).wait_recv()

            parts = [recv[half, v * QUAD + q, p * 16 : (p + 1) * 16, :] for p in range(2) for q in range(QUAD)]
            block = jnp.concatenate([part.astype(F32) for part in parts], 0).T
            for h in range(4):
                wh, ri = h // 2, h % 2
                start = pl.multiple_of(((half * 2 + ri) * 16 + v * 2 + wh) * REL_PITCH, 8)
                turned[pl.ds(start, 32), :] = block[h * 32 : (h + 1) * 32]
            return carry

        lax.fori_loop(0, WIN, one_block, 0)

        def gather(chunk, carry, half=half):
            for j in range(CHUNK):
                g = chunk * CHUNK + j
                real = turned[pl.ds(half * 32 * REL_PITCH + g, 16, stride=REL_PITCH), :]
                imag = turned[pl.ds((half * 32 + 16) * REL_PITCH + g, 16, stride=REL_PITCH), :]
                own[half, g] = jnp.concatenate([real, imag], 0).astype(BF16)
            halo_copy(0, half, chunk).start()
            halo_copy(1, half, chunk).start()
            return carry

        lax.fori_loop(0, CHUNKS, gather, 0)

    def operand(x, rx):
        def turn(u):
            return jnp.concatenate([u[16:32], -u[:16], u[48:], -u[32:48]], 0)

        return jnp.concatenate([jnp.where(left, x, turn(rx)), jnp.where(left, rx, turn(x))], 0).T.astype(BF16)

    def cross(chunk, carry):
        for way in range(2):
            for half in range(HALVES):
                halo_copy(way, half, chunk).wait_recv()
        for j in range(CHUNK):
            g = chunk * CHUNK + j
            a = jnp.concatenate([own[half, g].astype(F32) for half in range(HALVES)], 0)
            e = jnp.concatenate([halo[0, half, g].astype(F32) for half in range(HALVES)], 0)
            m = jnp.concatenate([halo[1, half, g].astype(F32) for half in range(HALVES)], 0)
            e = jnp.where(z + 1 < planes, e, 0.0)
            m = jnp.where(z > 0, m, 0.0)
            ra, re, rm = (pltpu.roll(x, 64, 1) for x in (a, e, m))
            right = jnp.concatenate([jnp.where(left, a, re), jnp.where(left, ra, e)], 0).astype(BF16)
            last = jnp.concatenate([e, re], 0).astype(BF16)
            for ref, value in (
                (near, jnp.dot(operand(a, ra), right, preferred_element_type=F32)),
                (far, jnp.dot(operand(m, rm), last, preferred_element_type=F32)),
            ):
                for part in range(2):
                    start = pl.multiple_of((g * 2 + part) * OUT_PITCH, 8)
                    ref[pl.ds(start, 64), :] = value[part * 64 : (part + 1) * 64]
        return carry

    lax.fori_loop(0, CHUNKS, cross, 0)

    def far_copy(to):
        return pltpu.make_async_remote_copy(
            src_ref=send_far.at[to],
            dst_ref=got_far.at[to],
            send_sem=f_send.at[to],
            recv_sem=f_recv.at[to],
            device_id=device(below, me),
            device_id_type=MESH,
        )

    def offsets_copy(ref, to, source):
        return pltpu.make_async_remote_copy(
            src_ref=ref.at[to],
            dst_ref=got.at[source],
            send_sem=x_send.at[to],
            recv_sem=x_recv.at[source],
            device_id=device(z, to),
            device_id_type=MESH,
        )

    def own_packet(ref):
        return pltpu.make_async_copy(ref.at[me], got.at[me], own_sem.at[HALVES])

    def ship(ref, to):
        @pl.when(to != me)
        def _():
            offsets_copy(ref, to, me).start()

        @pl.when(to == me)
        def _():
            own_packet(ref).start()

    wide = lax.broadcasted_iota(jnp.int32, (128, 128), 1) < 64

    def one_quarter(j, carry):
        q = (my_q + j) % QUAD

        def one_pair(i, carry):
            c = q * 16 + i
            for ref, column, base, size, target in (
                (near, near_col, 0, 128, send_near), (far, far_col, 128, 64, send_far)
            ):
                block = jnp.concatenate(
                    [ref[pl.ds(c, 64, stride=OUT_PITCH), :], ref[pl.ds(c + 8, 64, stride=OUT_PITCH), :]], 0
                )
                column[i, base : base + size, :] = block.T[:size]
                value = jnp.where(
                    wide, column[i, pl.ds(c + 1, 128), :], column[i, pl.ds(c + 9, 128), :]
                ).astype(BF16)
                rows = pl.ds(pl.multiple_of(i * 16, 16), 16)
                for v in range(WIN):
                    target[v * QUAD + q, rows, :] = value[v * 16 : (v + 1) * 16]
            return carry

        lax.fori_loop(0, 8, one_pair, 0, unroll=4)

        def one_send(k, carry):
            v = (my_v + k) % WIN
            to = v * QUAD + q

            @pl.when(v + q >= WIN - 1)
            def _():
                far_copy(to).start()

            @pl.when(v + q < WIN - 1)
            def _():
                ship(send_near, to)

            return carry

        lax.fori_loop(0, WIN, one_send, 0)
        return carry

    lax.fori_loop(0, QUAD, one_quarter, 0)

    def late_quarter(j, carry):
        q = (my_q + j) % QUAD

        def one_send(k, carry):
            v = (my_v + k) % WIN
            to = v * QUAD + q

            @pl.when(v + q >= WIN - 1)
            def _():
                far_copy(to).wait_recv()

            @pl.when(v + q == WIN - 1)
            def _():
                send_near[to] = (send_near[to].astype(F32) + got_far[to].astype(F32)).astype(BF16)
                ship(send_near, to)

            @pl.when(v + q >= WIN)
            def _():
                ship(got_far, to)

            return carry

        lax.fori_loop(0, WIN, one_send, 0)
        return carry

    lax.fori_loop(0, QUAD, late_quarter, 0)

    loads[5].wait()
    own_packet(send_near).wait()

    def arrived(j, carry):
        source = (me + j) % PLANE
        offsets_copy(send_near, source, source).wait_recv()
        return carry

    lax.fori_loop(1, PLANE, arrived, 0)

    def one_pair(f, carry):
        one, two = got[2 * f].astype(F32), got[2 * f + 1].astype(F32)
        span = pl.ds(pl.multiple_of(f * 128, 128), 128)
        lag_lhs[:128, span] = jnp.where(wide, one, pltpu.roll(two, 64, 1)).astype(BF16)
        lag_lhs[128:, span] = jnp.where(wide, pltpu.roll(one, 64, 1), two).astype(BF16)
        return carry

    lax.fori_loop(0, RADIX, one_pair, 0, unroll=8)
    for part in range(LAGS // 256):
        span = slice(part * 256, (part + 1) * 256)
        lags = jnp.dot(lag_lhs[...], table[:, span], preferred_element_type=F32) * scale
        for c in range(16):
            out[:, c, span] = lags[c * 16 : (c + 1) * 16]

    def drain(to, carry):
        @pl.when(to != me)
        def _():
            for half in range(HALVES):
                bins_copy(half, to, me).wait_send()
            offsets_copy(send_near, to, me).wait_send()

        @pl.when(to % QUAD + to // QUAD >= WIN - 1)
        def _():
            far_copy(to).wait_send()

        return carry

    lax.fori_loop(0, PLANE, drain, 0)

    def drain_halo(chunk, carry):
        for way in range(2):
            for half in range(HALVES):
                halo_copy(way, half, chunk).wait_send()
        return carry

    lax.fori_loop(0, CHUNKS, drain_halo, 0)


def body(planes, raw, offsets, mask):
    w_hi, w_lo = second_stage()
    tw_cos, tw_sin = twiddles()
    operands = [offsets, mask, raw, tw_cos, tw_sin, np.concatenate([w_hi, w_hi], 0), w_lo, lag_rows()]
    smem = pl.BlockSpec(memory_space=pltpu.SMEM)
    far_away = pl.BlockSpec(memory_space=pltpu.HBM)
    dma = pltpu.SemaphoreType.DMA
    vmem = pltpu.VMEM
    packets = vmem((PLANE, 128, 128), BF16)
    spectra = vmem((2 * BINS * OUT_PITCH, 128), F32)
    return pl.pallas_call(
        functools.partial(main_kernel, planes, 1.0 / math.sqrt(NB * 8 * WIN)),
        out_shape=jax.ShapeDtypeStruct((16, 16, LAGS), F32),
        in_specs=[smem, smem] + [far_away] * 6,
        out_specs=pl.BlockSpec(memory_space=pltpu.VMEM),
        scratch_shapes=[vmem(x.shape, x.dtype) for x in operands[2:]]
        + [
            vmem((RADIX, ROWS, 4 * TAIL), BF16),
            vmem((RADIX, ROWS, 128), F32),
            vmem((ROWS // 16, RADIX, 128), F32),
            vmem((ROWS // 16, RADIX, 128), F32),
            vmem((HALVES, PLANE, 32, 128), BF16),
            vmem((HALVES, PLANE, 32, 128), BF16),
            vmem((64 * REL_PITCH, 128), F32),
            vmem((HALVES, BINS, 32, 128), BF16),
            vmem((2, HALVES, BINS, 32, 128), BF16),
            spectra,
            spectra,
            vmem((SLOTS, 256, 128), F32),
            vmem((SLOTS, 256, 128), F32),
            packets,
            packets,
            packets,
            packets,
            vmem((256, 2 * NB), BF16),
            dma((6,)),
            dma((HALVES + 1,)),
            dma((HALVES, PLANE)),
            dma((HALVES, PLANE)),
            dma((2, HALVES, CHUNKS)),
            dma((2, HALVES, CHUNKS)),
            dma((PLANE,)),
            dma((PLANE,)),
            dma((PLANE,)),
            dma((PLANE,)),
        ],
        compiler_params=pltpu.CompilerParams(
            collective_id=0, has_side_effects=True, vmem_limit_bytes=48 * 2**20
        ),
        name="main",
    )(*(pltpu.with_memory_space_constraint(jnp.asarray(x), pltpu.HBM) for x in operands))


def solution(mesh):
    planes = mesh.shape["fibre"] // QUAD
    return jax.shard_map(
        functools.partial(body, planes),
        mesh=mesh,
        in_specs=(P("win", "fibre", None), P("win"), P("fibre")),
        out_specs=P("win", "fibre", None),
        check_vma=False,
    )
```

time: 65.7 us -> 53.5 us (0.81)
  Pallas kernels: 63.9 us -> 52.1 us
  local copies, waits for them, and re-layouts: 1.59 us -> 0.8 us
    pallas_call x2 -> x1, Pallas kernels: 63.9 us -> 52.1 us  [body(): pl.pallas_call(functools.partial(main_kernel, planes, 1.0 / math.sqrt(NB...]
    unnamed x2 -> x1, local copies, waits for them, and re-layouts: 1.59 us -> 0.8 us
where the time goes in v3:
time: 53.5 us; the launch traced here: 52.9 us
  Pallas kernels  52.1 us (97%)
  local copies, waits for them, and re-layouts  0.8 us (1%)
    pallas_call x1, Pallas kernels, body(): pl.pallas_call(functools.partial(main_kernel, planes, 1.0 / math.sqrt(NB...  52.1 us

profile of v3, /device:TPU:1, one launch (start us, length us, event | category | flops | bytes accessed | tf_op | source)
XLA Modules:
  0.0 52.9 jit_solution(10999176594810012100)
XLA Ops:
  0.0 52.1 %main.1 = f32[16,16,512]{2,1,0:T(8,128)S(1)} custom-call(s32[8]{0:T(128)} %offsets.1, s32[16]{0:T(128)} %mask.1, bf16[8,16,4352]{2,1,0:T(8,128)(2,1)} %raw_hbm.1, f32[16,256]{1,0:T(8,128)} %constant.10.clone.cos_hbm, f32[16,256]{1,0:T(8,128)} %constant.11.clone.sin_hbm, bf16[1024,256]{1,0:T(8,128)(2,1)} %constant.12.clone.hi_hbm, ...), custom_call_target="tpu_custom_call" | custom-call | tf_op jit(solution)/shard_map/main/pallas_call | solution.py:516
  52.1 0.8 %copy.10 = f32[16,16,512]{2,1,0:T(8,128)} copy(f32[16,16,512]{2,1,0:T(8,128)S(1)} %main.1) | data formatting | bytes 1048576

commit v4 on v3

v4 whole, which is shorter than its diff:
```python
import functools
import math

import jax
import jax.numpy as jnp
import numpy as np
from jax import lax
from jax.experimental import pallas as pl
from jax.experimental.pallas import tpu as pltpu
from jax.sharding import PartitionSpec as P

MESH = pl.DeviceIdType.MESH
L = 4096
BAND_LO = 64
NB = 1024
SMOOTH = 64
LAGS = 512
SPAN = 128
EPS = 1e-06
RADIX = 16
TAIL = L // RADIX
PLANE = 32
WIN = 8
QUAD = 4
BINS = 32
CHUNK = 8
REL_PITCH = 40
OUT_PITCH = 72
SLOTS = 8
HALVES = 2
ROWS = 128 // HALVES
CHUNKS = BINS // CHUNK
MEAN_UNROLL = 4
FFT_UNROLL = 2
GROUP = 16
F32 = jnp.float32
BF16 = jnp.bfloat16


def second_stage():
    b = np.arange(TAIL)[:, None]
    lane = np.arange(128)[None, :]
    half, imag, low = lane // 64, (lane // 32) % 2, lane % 32
    angle = 2.0 * np.pi * ((b * (BAND_LO // RADIX + half * 32 + low)) % TAIL) / TAIL
    cos, sin = np.cos(angle), np.sin(angle)
    whole = np.where(imag == 0, np.concatenate([cos, sin], 0), np.concatenate([-sin, cos], 0)).astype(np.float32)
    high = whole.astype(jnp.bfloat16)
    return np.concatenate([high, (whole - high.astype(np.float32)).astype(jnp.bfloat16)], 1)


def first_tables():
    f = np.arange(RADIX)[:, None]
    b = np.arange(TAIL)[None, :]
    twiddle, spot = 2.0 * np.pi * (f * b) / L, 2.0 * np.pi * (TAIL * f + b) / L
    return np.stack([np.cos(twiddle), np.sin(twiddle), np.cos(spot), np.sin(spot)]).astype(np.float32)


def lag_rows():
    frequency = np.arange(NB, dtype=np.int64) + BAND_LO
    lag_index = np.arange(LAGS, dtype=np.int64) - LAGS // 2
    turns = np.mod(frequency[:, None] * lag_index[None, :], L).astype(np.float32)
    angles = turns * np.float32(2.0 * math.pi / L)
    cos, sin = np.cos(angles.astype(np.float64)), np.sin(angles.astype(np.float64))
    table = np.stack([cos, -sin], 1).astype(np.float32)
    bins = RADIX * np.arange(64)[None, :] + np.arange(RADIX)[:, None]
    return table[bins].reshape(2 * NB, LAGS).astype(jnp.bfloat16)


def real_fft(x):
    n = len(x)
    if n == 2:
        return [(x[0] + x[1], None), (x[0] - x[1], None)]
    even, odd = real_fft(x[0::2]), real_fft(x[1::2])
    half, quarter = n // 2, n // 4
    out = [None] * (half + 1)
    out[0] = (even[0][0] + odd[0][0], None)
    out[half] = (even[0][0] - odd[0][0], None)
    for k in range(1, quarter):
        (er, ei), (orr, oi) = even[k], odd[k]
        c, s = math.cos(2.0 * math.pi * k / n), math.sin(2.0 * math.pi * k / n)
        if 8 * k == n:
            tr, ti = (orr + oi) * c, (oi - orr) * c
        else:
            tr, ti = orr * c + oi * s, oi * c - orr * s
        out[k] = (er + tr, ei + ti)
        out[half - k] = (er - tr, ti - ei)
    out[quarter] = (even[quarter][0], -odd[quarter][0])
    return out


def place():
    fibre, win = lax.axis_index("fibre"), lax.axis_index("win")
    return fibre // QUAD, win * QUAD + fibre % QUAD


def device(z, s):
    return (z * QUAD + s % QUAD, s // QUAD)


def greet_all(planes, z, me):
    barrier = pltpu.get_barrier_semaphore()

    def signal(plane, s):
        pl.semaphore_signal(barrier, inc=1, device_id=device(plane, s), device_id_type=MESH)

    def near(j, carry):
        signal(z, (me + j) % PLANE)
        return carry

    lax.fori_loop(1, PLANE, near, 0)
    signal((z + 1) % planes, me)
    signal((z + planes - 1) % planes, me)
    return PLANE - 1 + 2


def window_of(half, i):
    return (i // 2) * 4 + half * 2 + i % 2


def shifts(offsets, turn_f, turn_g):
    def one_window(w, carry):
        f = lax.broadcasted_iota(jnp.int32, (RADIX, 128), 0)
        angle = ((f * offsets[w]) & (L - 1)).astype(F32) * (2.0 * math.pi / L)
        turn_f[0, w] = jnp.cos(angle)
        turn_f[1, w] = jnp.sin(angle)
        return carry

    lax.fori_loop(0, 8, one_window, 0, unroll=2)
    row = lax.broadcasted_iota(jnp.int32, (8, 128), 0)
    lane = lax.broadcasted_iota(jnp.int32, (8, 128), 1)
    start = jnp.zeros((8, 128), jnp.int32)
    for w in range(8):
        start = jnp.where(row == w, offsets[w], start)
    k = (BAND_LO // RADIX + (lane // 64) * 32 + lane % 32) * RADIX
    angle = ((k * start) & (L - 1)).astype(F32) * (2.0 * math.pi / L)
    turn_g[0] = jnp.cos(angle)
    turn_g[1] = jnp.where((lane // 32) % 2 == 0, -jnp.sin(angle), jnp.sin(angle))


def first_stage(half, offsets, raw, tables, lhs, turn_f, means):
    width = 128
    lane = lax.broadcasted_iota(jnp.int32, (16, width), 1)

    def sample(w, a, low):
        here = raw[w, :, pl.ds(a * TAIL + low, width)].astype(F32)
        if a:
            return here
        return jnp.where(lane + low < offsets[w], raw[w, :, pl.ds(L + low, width)].astype(F32), here)

    def one_mean(i, carry):
        w = window_of(half, i)
        total = functools.reduce(lambda p, q: p + q, [sample(w, a, low) for a in range(RADIX) for low in (0, width)])
        means[i] = jnp.broadcast_to(jnp.sum(total, axis=1, keepdims=True) * (1.0 / L), (16, width))
        return carry

    lax.fori_loop(0, ROWS // 16, one_mean, 0, unroll=MEAN_UNROLL)

    def one_window(index, carry):
        i, column = index // 2, index % 2
        w = window_of(half, i)
        mean = means[i]
        rows = pl.ds(pl.multiple_of(i * 16, 16), 16)
        low = pl.multiple_of(column * width, width)
        span = pl.ds(low, width)
        turn_cos, turn_sin = turn_f[0, w], turn_f[1, w]
        cosine, sine = tables[0, :, span], tables[1, :, span]
        cosine, sine = cosine * turn_cos + sine * turn_sin, sine * turn_cos - cosine * turn_sin
        taper = 0.5 - 0.5 * (tables[2, :, span] * turn_cos[1:2] + tables[3, :, span] * turn_sin[1:2])
        spectrum = real_fft([(sample(w, a, low) - mean) * taper[a : a + 1] for a in range(RADIX)])
        for f in range(RADIX):
            re, im = spectrum[f] if f <= RADIX // 2 else spectrum[RADIX - f]
            if f > RADIX // 2:
                im = -im
            if f:
                c, s = cosine[f : f + 1], sine[f : f + 1]
                re, im = (re * c, -re * s) if im is None else (re * c + im * s, im * c - re * s)
            else:
                im = jnp.zeros_like(re)
            for part, value in enumerate((re, im)):
                high = value.astype(BF16)
                lhs[f, rows, pl.ds(low + part * TAIL, width)] = high
                lhs[f, rows, pl.ds(low + (2 + part) * TAIL, width)] = (value - high.astype(F32)).astype(BF16)
        return carry

    lax.fori_loop(0, ROWS // 8, one_window, 0, unroll=FFT_UNROLL)


def second_stage_of(half, lhs, weights, kept, turn_g):
    lane = lax.broadcasted_iota(jnp.int32, (ROWS, 128), 1)
    real = (lane // 32) % 2 == 0
    turn = [
        jnp.concatenate(
            [jnp.broadcast_to(turn_g[part, w : w + 1], (16, 128)) for w in (window_of(half, i) for i in range(ROWS // 16))],
            0,
        )
        for part in range(2)
    ]
    power = jnp.zeros((ROWS, 128), F32)
    for start in range(0, RADIX, GROUP):
        whole = lhs[start : start + GROUP].reshape(GROUP * ROWS, 4 * TAIL)
        first = jnp.dot(whole[:, : 2 * TAIL], weights[...], preferred_element_type=F32)
        second = jnp.dot(whole[:, 2 * TAIL :], weights[:, :128], preferred_element_type=F32)
        both = (first[:, :128] + first[:, 128:] + second).reshape(GROUP, ROWS, 128)
        for j in range(GROUP):
            one = both[j]
            power = power + one * one
            other = jnp.where(real, pltpu.roll(one, 96, 1), pltpu.roll(one, 32, 1))
            kept[start + j] = one * turn[0] + other * turn[1]
    return power


def whitening(power, mask):
    row = lax.broadcasted_iota(jnp.int32, (128, 128), 0)
    col = lax.broadcasted_iota(jnp.int32, (128, 128), 1)
    same = (row // 64 == col // 64) & ((row % 32) // 4 == (col % 32) // 4)
    block = jnp.where(same, 1.0, 0.0).astype(F32)
    mean_power = jnp.dot(power, block, precision=lax.Precision.HIGHEST, preferred_element_type=F32) * (1.0 / SMOOTH)
    channel = lax.broadcasted_iota(jnp.int32, (16, 128), 0)
    flag = jnp.zeros((16, 128), F32)
    for c in range(16):
        flag = jnp.where(channel == c, mask[c].astype(F32), flag)
    flag = jnp.broadcast_to(flag[None], (ROWS // 16, 16, 128)).reshape(ROWS, 128)
    return (1.0 / jnp.sqrt(mean_power + EPS)) * flag


def main_kernel(
    planes, scale, offsets, mask, raw_hbm, tables_hbm, weights_hbm, table_hbm, out,
    raw, tables, weights, table, lhs, kept, turn_f, turn_g, means,
    send, recv, turned, own, halo, near, far, near_col, far_col, send_near, send_far, got_far, got, lag_lhs,
    in_sem, own_sem, s_send, s_recv, h_send, h_recv, x_send, x_recv, f_send, f_recv,
):
    z, me = place()
    my_q, my_v = me % QUAD, me // QUAD
    above, below = (z + 1) % planes, (z + planes - 1) % planes
    pairs = [
        (raw_hbm.at[pl.ds(start, 2)], raw.at[pl.ds(start, 2)]) for start in (0, 4, 2, 6)
    ] + [(tables_hbm, tables), (weights_hbm, weights), (table_hbm, table)]
    pairs = [pairs[i] for i in (4, 0, 1, 2, 3, 5, 6)]
    loads = [pltpu.make_async_copy(source, target, in_sem.at[i]) for i, (source, target) in enumerate(pairs)]
    for load in loads[:6]:
        load.start()
    expected = greet_all(planes, z, me)
    shifts(offsets, turn_f, turn_g)
    for slot in range(SLOTS):
        near_col[slot, 128:, :] = jnp.zeros((128, 128), F32)
        far_col[slot, :128, :] = jnp.zeros((128, 128), F32)
    left = lax.broadcasted_iota(jnp.int32, (64, 128), 1) < 64

    def bins_copy(half, to, source):
        return pltpu.make_async_remote_copy(
            src_ref=send.at[half, to],
            dst_ref=recv.at[half, source],
            send_sem=s_send.at[half],
            recv_sem=s_recv.at[half],
            device_id=device(z, to),
            device_id_type=MESH,
        )

    def all_bins(half):
        return pltpu.make_async_remote_copy(
            src_ref=send.at[half, pl.ds(0, PLANE - 1)],
            dst_ref=recv.at[half, pl.ds(0, PLANE - 1)],
            send_sem=s_send.at[half],
            recv_sem=s_recv.at[half],
            device_id=device(z, (me + 1) % PLANE),
            device_id_type=MESH,
        )

    def own_copy(half):
        return pltpu.make_async_copy(send.at[half, me], recv.at[half, me], own_sem.at[half])

    for half in range(HALVES):
        for load in loads[:3] if half == 0 else loads[3:5]:
            load.wait()
        first_stage(half, offsets, raw, tables, lhs, turn_f, means)
        if half == 0:
            loads[5].wait()
        factor = whitening(second_stage_of(half, lhs, weights, kept, turn_g), mask)
        if half == 0:
            pl.semaphore_wait(pltpu.get_barrier_semaphore(), expected)

        for f in range(RADIX):
            value = kept[f] * factor
            top, bottom = value[:32], value[32:]
            send[half, 2 * f] = jnp.where(left[:32], top, pltpu.roll(bottom, 64, 1)).astype(BF16)
            send[half, 2 * f + 1] = jnp.where(left[:32], pltpu.roll(top, 64, 1), bottom).astype(BF16)
        own_copy(half).start()

        def launch(j, carry, half=half):
            bins_copy(half, (me + j) % PLANE, me).start()
            return carry

        lax.fori_loop(1, PLANE, launch, 0)

    loads[6].start()

    def halo_copy(way, half, chunk):
        span = pl.ds(chunk * CHUNK, CHUNK)
        return pltpu.make_async_remote_copy(
            src_ref=own.at[half, span],
            dst_ref=halo.at[way, half, span],
            send_sem=h_send.at[way, half, chunk],
            recv_sem=h_recv.at[way, half, chunk],
            device_id=device(below if way == 0 else above, me),
            device_id_type=MESH,
        )

    for half in range(HALVES):
        own_copy(half).wait()
        all_bins(half).wait_recv()

        def one_block(v, carry, half=half):
            parts = [recv[half, v * QUAD + q, p * 16 : (p + 1) * 16, :] for p in range(2) for q in range(QUAD)]
            block = jnp.concatenate([part.astype(F32) for part in parts], 0).T
            for h in range(4):
                wh, ri = h // 2, h % 2
                start = pl.multiple_of(((half * 2 + ri) * 16 + v * 2 + wh) * REL_PITCH, 8)
                turned[pl.ds(start, 32), :] = block[h * 32 : (h + 1) * 32]
            return carry

        lax.fori_loop(0, WIN, one_block, 0, unroll=4)

        def gather(chunk, carry, half=half):
            for j in range(CHUNK):
                g = chunk * CHUNK + j
                real = turned[pl.ds(half * 32 * REL_PITCH + g, 16, stride=REL_PITCH), :]
                imag = turned[pl.ds((half * 32 + 16) * REL_PITCH + g, 16, stride=REL_PITCH), :]
                own[half, g] = jnp.concatenate([real, imag], 0).astype(BF16)
            halo_copy(0, half, chunk).start()
            halo_copy(1, half, chunk).start()
            return carry

        lax.fori_loop(0, CHUNKS, gather, 0)

    for half in range(HALVES):
        all_bins(half).wait_send()

    def operand(x, rx):
        def turn(u):
            return jnp.concatenate([u[16:32], -u[:16], u[48:], -u[32:48]], 0)

        return jnp.concatenate([jnp.where(left, x, turn(rx)), jnp.where(left, rx, turn(x))], 0).T.astype(BF16)

    def cross(chunk, carry):
        for way in range(2):
            for half in range(HALVES):
                halo_copy(way, half, chunk).wait_recv()
        for j in range(CHUNK):
            g = chunk * CHUNK + j
            a = jnp.concatenate([own[half, g].astype(F32) for half in range(HALVES)], 0)
            e = jnp.concatenate([halo[0, half, g].astype(F32) for half in range(HALVES)], 0)
            m = jnp.concatenate([halo[1, half, g].astype(F32) for half in range(HALVES)], 0)
            e = jnp.where(z + 1 < planes, e, 0.0)
            m = jnp.where(z > 0, m, 0.0)
            ra, re, rm = (pltpu.roll(x, 64, 1) for x in (a, e, m))
            right = jnp.concatenate([jnp.where(left, a, re), jnp.where(left, ra, e)], 0).astype(BF16)
            last = jnp.concatenate([e, re], 0).astype(BF16)
            for ref, value in (
                (near, jnp.dot(operand(a, ra), right, preferred_element_type=F32)),
                (far, jnp.dot(operand(m, rm), last, preferred_element_type=F32)),
            ):
                for part in range(2):
                    start = pl.multiple_of((g * 2 + part) * OUT_PITCH, 8)
                    ref[pl.ds(start, 64), :] = value[part * 64 : (part + 1) * 64]
        return carry

    lax.fori_loop(0, CHUNKS, cross, 0)

    def far_copy(to):
        return pltpu.make_async_remote_copy(
            src_ref=send_far.at[to],
            dst_ref=got_far.at[to],
            send_sem=f_send.at[to],
            recv_sem=f_recv.at[to],
            device_id=device(below, me),
            device_id_type=MESH,
        )

    def offsets_copy(ref, to, source):
        return pltpu.make_async_remote_copy(
            src_ref=ref.at[to],
            dst_ref=got.at[source],
            send_sem=x_send.at[0],
            recv_sem=x_recv.at[0],
            device_id=device(z, to),
            device_id_type=MESH,
        )

    def all_offsets():
        return pltpu.make_async_remote_copy(
            src_ref=send_near.at[pl.ds(0, PLANE - 1)],
            dst_ref=got.at[pl.ds(0, PLANE - 1)],
            send_sem=x_send.at[0],
            recv_sem=x_recv.at[0],
            device_id=device(z, (me + 1) % PLANE),
            device_id_type=MESH,
        )

    def own_packet(ref):
        return pltpu.make_async_copy(ref.at[me], got.at[me], own_sem.at[HALVES])

    def ship(ref, to):
        @pl.when(to != me)
        def _():
            offsets_copy(ref, to, me).start()

        @pl.when(to == me)
        def _():
            own_packet(ref).start()

    wide = lax.broadcasted_iota(jnp.int32, (128, 128), 1) < 64

    def pair_of(ref, column, base, size, target, q):
        def one_pair(i, carry):
            c = q * 16 + i
            block = jnp.concatenate(
                [ref[pl.ds(c, 64, stride=OUT_PITCH), :], ref[pl.ds(c + 8, 64, stride=OUT_PITCH), :]], 0
            )
            column[i, base : base + size, :] = block.T[:size]
            value = jnp.where(
                wide, column[i, pl.ds(c + 1, 128), :], column[i, pl.ds(c + 9, 128), :]
            ).astype(BF16)
            rows = pl.ds(pl.multiple_of(i * 16, 16), 16)
            for v in range(WIN):
                target[v * QUAD + q, rows, :] = value[v * 16 : (v + 1) * 16]
            return carry

        lax.fori_loop(0, 8, one_pair, 0, unroll=4)

    def far_quarter(j, carry):
        q = (my_q + j) % QUAD
        pair_of(far, far_col, 128, 64, send_far, q)

        def one_send(k, carry):
            far_copy((WIN - 1 - k) * QUAD + q).start()
            return carry

        lax.fori_loop(0, q + 1, one_send, 0)
        return carry

    lax.fori_loop(0, QUAD, far_quarter, 0)

    def near_quarter(j, carry):
        q = (my_q + j) % QUAD
        pair_of(near, near_col, 0, 128, send_near, q)

        def one_send(k, carry):
            v = (my_v + k) % WIN

            @pl.when(v + q < WIN - 1)
            def _():
                ship(send_near, v * QUAD + q)

            return carry

        lax.fori_loop(0, WIN, one_send, 0)
        return carry

    lax.fori_loop(0, QUAD, near_quarter, 0)

    def late_quarter(j, carry):
        q = (my_q + j) % QUAD

        def one_send(k, carry):
            to = (WIN - 1 - k) * QUAD + q
            far_copy(to).wait_recv()

            @pl.when(k == q)
            def _():
                send_near[to] = (send_near[to].astype(F32) + got_far[to].astype(F32)).astype(BF16)
                ship(send_near, to)

            @pl.when(k != q)
            def _():
                ship(got_far, to)

            return carry

        lax.fori_loop(0, q + 1, one_send, 0)
        return carry

    lax.fori_loop(0, QUAD, late_quarter, 0)

    def drain_halo(chunk, carry):
        for way in range(2):
            for half in range(HALVES):
                halo_copy(way, half, chunk).wait_send()
        return carry

    lax.fori_loop(0, CHUNKS, drain_halo, 0)

    def drain_far(q, carry):
        def one(k, carry):
            far_copy((WIN - 1 - k) * QUAD + q).wait_send()
            return carry

        return lax.fori_loop(0, q + 1, one, carry)

    lax.fori_loop(0, QUAD, drain_far, 0)
    loads[6].wait()
    own_packet(send_near).wait()
    all_offsets().wait()

    for f in range(RADIX):
        one, two = got[2 * f].astype(F32), got[2 * f + 1].astype(F32)
        span = slice(f * 128, (f + 1) * 128)
        lag_lhs[:128, span] = jnp.where(wide, one, pltpu.roll(two, 64, 1)).astype(BF16)
        lag_lhs[128:, span] = jnp.where(wide, pltpu.roll(one, 64, 1), two).astype(BF16)
    lags = jnp.dot(lag_lhs[...], table[...], preferred_element_type=F32) * scale
    for c in range(16):
        out[:, c, :] = lags[c * 16 : (c + 1) * 16]


def body(planes, raw, offsets, mask):
    operands = [offsets, mask, raw, first_tables(), second_stage(), lag_rows()]
    smem = pl.BlockSpec(memory_space=pltpu.SMEM)
    far_away = pl.BlockSpec(memory_space=pltpu.HBM)
    dma = pltpu.SemaphoreType.DMA
    vmem = pltpu.VMEM
    packets = vmem((PLANE, 128, 128), BF16)
    spectra = vmem((2 * BINS * OUT_PITCH, 128), F32)
    return pl.pallas_call(
        functools.partial(main_kernel, planes, 1.0 / math.sqrt(NB * 8 * WIN)),
        out_shape=jax.ShapeDtypeStruct((16, 16, LAGS), F32),
        in_specs=[smem, smem] + [far_away] * 4,
        out_specs=pl.BlockSpec(memory_space=pltpu.VMEM),
        scratch_shapes=[vmem(x.shape, x.dtype) for x in operands[2:]]
        + [
            vmem((RADIX, ROWS, 4 * TAIL), BF16),
            vmem((RADIX, ROWS, 128), F32),
            vmem((2, 8, RADIX, 128), F32),
            vmem((2, 8, 128), F32),
            vmem((ROWS // 16, 16, 128), F32),
            vmem((HALVES, PLANE, 32, 128), BF16),
            vmem((HALVES, PLANE, 32, 128), BF16),
            vmem((64 * REL_PITCH, 128), F32),
            vmem((HALVES, BINS, 32, 128), BF16),
            vmem((2, HALVES, BINS, 32, 128), BF16),
            spectra,
            spectra,
            vmem((SLOTS, 256, 128), F32),
            vmem((SLOTS, 256, 128), F32),
            packets,
            packets,
            packets,
            packets,
            vmem((256, 2 * NB), BF16),
            dma((7,)),
            dma((HALVES + 1,)),
            dma((HALVES,)),
            dma((HALVES,)),
            dma((2, HALVES, CHUNKS)),
            dma((2, HALVES, CHUNKS)),
            dma((1,)),
            dma((1,)),
            dma((PLANE,)),
            dma((PLANE,)),
        ],
        compiler_params=pltpu.CompilerParams(
            collective_id=0, has_side_effects=True, vmem_limit_bytes=48 * 2**20
        ),
        name="main",
    )(*(pltpu.with_memory_space_constraint(jnp.asarray(x), pltpu.HBM) for x in operands))


def solution(mesh):
    planes = mesh.shape["fibre"] // QUAD
    return jax.shard_map(
        functools.partial(body, planes),
        mesh=mesh,
        in_specs=(P("win", "fibre", None), P("win"), P("fibre")),
        out_specs=P("win", "fibre", None),
        check_vma=False,
    )
```

time: 53.5 us -> 51.2 us (0.957)
  Pallas kernels: 52.1 us -> 49.7 us
    pallas_call x1, Pallas kernels: 52.1 us -> 49.7 us  [body(): pl.pallas_call(functools.partial(main_kernel, planes, 1.0 / math.sqrt(NB...]
where the time goes in v4:
time: 51.2 us; the launch traced here: 50.5 us
  Pallas kernels  49.7 us (97%)
  local copies, waits for them, and re-layouts  0.8 us (2%)
    pallas_call x1, Pallas kernels, body(): pl.pallas_call(functools.partial(main_kernel, planes, 1.0 / math.sqrt(NB...  49.7 us

profile of v4, /device:TPU:1, one launch (start us, length us, event | category | flops | bytes accessed | tf_op | source)
XLA Modules:
  0.0 50.5 jit_solution(8439606112456723114)
XLA Ops:
  0.0 49.7 %main.1 = f32[16,16,512]{2,1,0:T(8,128)S(1)} custom-call(s32[8]{0:T(128)} %offsets.1, s32[16]{0:T(128)} %mask.1, bf16[8,16,4352]{2,1,0:T(8,128)(2,1)} %raw_hbm.1, f32[4,16,256]{2,1,0:T(8,128)} %constant.6.clone.tables_hbm, bf16[512,256]{1,0:T(8,128)(2,1)} %constant.7.clone.weights_hbm, bf16[2048,512]{1,0:T(8,128)(2,1)} %constant.8.clone.table_hbm), custom_call_target="tpu_custom_call" | custom-call | tf_op jit(solution)/shard_map/main/pallas_call | solution.py:522
  49.8 0.8 %copy.8 = f32[16,16,512]{2,1,0:T(8,128)} copy(f32[16,16,512]{2,1,0:T(8,128)S(1)} %main.1) | data formatting | bytes 1048576

commit v5 on v4

--- a/solution.py
+++ b/solution.py
@@ -26,7 +26,8 @@
 CHUNK = 8
 REL_PITCH = 40
 OUT_PITCH = 72
-SLOTS = 8
+SLOTS = 4
+FARTHEST_FIRST = ((1, 2), (1, 1), (1, 3), (1, 0), (0, 2), (0, 1), (0, 3), (0, 0))
 HALVES = 2
 ROWS = 128 // HALVES
 CHUNKS = BINS // CHUNK
@@ -63,7 +64,8 @@
     cos, sin = np.cos(angles.astype(np.float64)), np.sin(angles.astype(np.float64))
     table = np.stack([cos, -sin], 1).astype(np.float32)
     bins = RADIX * np.arange(64)[None, :] + np.arange(RADIX)[:, None]
-    return table[bins].reshape(2 * NB, LAGS).astype(jnp.bfloat16)
+    table = table[bins].reshape(RADIX, 2, 2, 16, 2, LAGS)
+    return table.transpose(2, 0, 1, 3, 4, 5).reshape(2 * NB, LAGS).astype(jnp.bfloat16)
 
 
 def real_fft(x):
@@ -226,7 +228,7 @@
 def main_kernel(
     planes, scale, offsets, mask, raw_hbm, tables_hbm, weights_hbm, table_hbm, out,
     raw, tables, weights, table, lhs, kept, turn_f, turn_g, means,
-    send, recv, turned, own, halo, near, far, near_col, far_col, send_near, send_far, got_far, got, lag_lhs,
+    send, recv, turned, own, halo, near, far, near_col, far_col, send_own, send_near, send_far, got_far, got, lag_lhs, first_lags, own_left,
     in_sem, own_sem, s_send, s_recv, h_send, h_recv, x_send, x_recv, f_send, f_recv,
 ):
     z, me = place()
@@ -286,11 +288,14 @@
             send[half, 2 * f + 1] = jnp.where(left[:32], pltpu.roll(top, 64, 1), bottom).astype(BF16)
         own_copy(half).start()
 
-        def launch(j, carry, half=half):
-            bins_copy(half, (me + j) % PLANE, me).start()
-            return carry
-
-        lax.fori_loop(1, PLANE, launch, 0)
+        for far_x, far_y in FARTHEST_FIRST:
+
+            def launch(j, carry, half=half, far_x=far_x, far_y=far_y):
+                to = ((my_v // 4 + far_x) % 2 * 4 + (my_v + far_y) % 4) * QUAD + (my_q + j) % QUAD
+                bins_copy(half, to, me).start()
+                return carry
+
+            lax.fori_loop(0 if far_x + far_y else 1, QUAD, launch, 0)
 
     loads[6].start()
 
@@ -341,13 +346,31 @@
 
         return jnp.concatenate([jnp.where(left, x, turn(rx)), jnp.where(left, rx, turn(x))], 0).T.astype(BF16)
 
+    def own_rows(g):
+        return jnp.concatenate([own[half, g].astype(F32) for half in range(HALVES)], 0)
+
+    def keep(ref, g, value):
+        for part in range(2):
+            start = pl.multiple_of((g * 2 + part) * OUT_PITCH, 8)
+            ref[pl.ds(start, 64), :] = value[part * 64 : (part + 1) * 64]
+
+    def own_operand(g, carry):
+        a = own_rows(g)
+        ra = pltpu.roll(a, 64, 1)
+        mine = operand(a, ra)
+        own_left[g] = mine
+        keep(near, g, jnp.dot(mine, jnp.concatenate([a, ra], 0).astype(BF16), preferred_element_type=F32))
+        return carry
+
+    lax.fori_loop(0, BINS, own_operand, 0, unroll=4)
+
     def cross(chunk, carry):
         for way in range(2):
             for half in range(HALVES):
                 halo_copy(way, half, chunk).wait_recv()
         for j in range(CHUNK):
             g = chunk * CHUNK + j
-            a = jnp.concatenate([own[half, g].astype(F32) for half in range(HALVES)], 0)
+            a = own_rows(g)
             e = jnp.concatenate([halo[0, half, g].astype(F32) for half in range(HALVES)], 0)
             m = jnp.concatenate([halo[1, half, g].astype(F32) for half in range(HALVES)], 0)
             e = jnp.where(z + 1 < planes, e, 0.0)
@@ -355,131 +378,147 @@
             ra, re, rm = (pltpu.roll(x, 64, 1) for x in (a, e, m))
             right = jnp.concatenate([jnp.where(left, a, re), jnp.where(left, ra, e)], 0).astype(BF16)
             last = jnp.concatenate([e, re], 0).astype(BF16)
-            for ref, value in (
-                (near, jnp.dot(operand(a, ra), right, preferred_element_type=F32)),
-                (far, jnp.dot(operand(m, rm), last, preferred_element_type=F32)),
-            ):
-                for part in range(2):
-                    start = pl.multiple_of((g * 2 + part) * OUT_PITCH, 8)
-                    ref[pl.ds(start, 64), :] = value[part * 64 : (part + 1) * 64]
+            keep(near, g, jnp.dot(own_left[g], right, preferred_element_type=F32))
+            keep(far, g, jnp.dot(operand(m, rm), last, preferred_element_type=F32))
         return carry
 
-    lax.fori_loop(0, CHUNKS, cross, 0)
-
-    def far_copy(to):
+    def far_copy(part, to):
         return pltpu.make_async_remote_copy(
-            src_ref=send_far.at[to],
-            dst_ref=got_far.at[to],
-            send_sem=f_send.at[to],
-            recv_sem=f_recv.at[to],
+            src_ref=send_far.at[part, to],
+            dst_ref=got_far.at[part, to],
+            send_sem=f_send.at[part, to],
+            recv_sem=f_recv.at[part, to],
             device_id=device(below, me),
             device_id_type=MESH,
         )
 
-    def offsets_copy(ref, to, source):
+    def offsets_copy(ref, part, to):
         return pltpu.make_async_remote_copy(
-            src_ref=ref.at[to],
-            dst_ref=got.at[source],
-            send_sem=x_send.at[0],
-            recv_sem=x_recv.at[0],
+            src_ref=ref.at[part, to],
+            dst_ref=got.at[part, me],
+            send_sem=x_send.at[part],
+            recv_sem=x_recv.at[part],
             device_id=device(z, to),
             device_id_type=MESH,
         )
 
-    def all_offsets():
+    def all_offsets(part):
         return pltpu.make_async_remote_copy(
-            src_ref=send_near.at[pl.ds(0, PLANE - 1)],
-            dst_ref=got.at[pl.ds(0, PLANE - 1)],
-            send_sem=x_send.at[0],
-            recv_sem=x_recv.at[0],
+            src_ref=send_near.at[part, pl.ds(0, PLANE - 1)],
+            dst_ref=got.at[part, pl.ds(0, PLANE - 1)],
+            send_sem=x_send.at[part],
+            recv_sem=x_recv.at[part],
             device_id=device(z, (me + 1) % PLANE),
             device_id_type=MESH,
         )
 
-    def own_packet(ref):
-        return pltpu.make_async_copy(ref.at[me], got.at[me], own_sem.at[HALVES])
-
-    def ship(ref, to):
+    def own_packet(ref, part):
+        return pltpu.make_async_copy(ref.at[part, me], got.at[part, me], own_sem.at[HALVES + part])
+
+    def ship(ref, part, to):
         @pl.when(to != me)
         def _():
-            offsets_copy(ref, to, me).start()
+            offsets_copy(ref, part, to).start()
 
         @pl.when(to == me)
         def _():
-            own_packet(ref).start()
-
-    wide = lax.broadcasted_iota(jnp.int32, (128, 128), 1) < 64
-
-    def pair_of(ref, column, base, size, target, q):
-        def one_pair(i, carry):
+            own_packet(ref, part).start()
+
+    lane = lax.broadcasted_iota(jnp.int32, (128, 128), 1)
+
+    def packets_of(ref, column, base, size, target, part, q):
+        def one_group(i, carry):
             c = q * 16 + i
+            start = part * BINS * OUT_PITCH
             block = jnp.concatenate(
-                [ref[pl.ds(c, 64, stride=OUT_PITCH), :], ref[pl.ds(c + 8, 64, stride=OUT_PITCH), :]], 0
+                [ref[pl.ds(start + c + 4 * k, BINS, stride=OUT_PITCH), :] for k in range(4)], 0
             )
             column[i, base : base + size, :] = block.T[:size]
-            value = jnp.where(
-                wide, column[i, pl.ds(c + 1, 128), :], column[i, pl.ds(c + 9, 128), :]
-            ).astype(BF16)
+            value = column[i, pl.ds(c + 13, 128), :]
+            for k in (2, 1, 0):
+                value = jnp.where(lane < 32 * k + 32, column[i, pl.ds(c + 4 * k + 1, 128), :], value)
+            value = value.astype(BF16)
             rows = pl.ds(pl.multiple_of(i * 16, 16), 16)
             for v in range(WIN):
-                target[v * QUAD + q, rows, :] = value[v * 16 : (v + 1) * 16]
+                target[part, v * QUAD + q, rows, :] = value[v * 16 : (v + 1) * 16]
             return carry
 
-        lax.fori_loop(0, 8, one_pair, 0, unroll=4)
-
-    def far_quarter(j, carry):
-        q = (my_q + j) % QUAD
-        pair_of(far, far_col, 128, 64, send_far, q)
-
-        def one_send(k, carry):
-            far_copy((WIN - 1 - k) * QUAD + q).start()
+        lax.fori_loop(0, 4, one_group, 0, unroll=4)
+
+    def early_part(part, carry):
+        def early_quarter(q, carry):
+            packets_of(near, near_col, 0, 128, send_own, part, q)
+            for far_x, far_y in FARTHEST_FIRST:
+                v = (my_v // 4 + far_x) % 2 * 4 + (my_v + far_y) % 4
+
+                @pl.when(v + q < 3)
+                def _(v=v):
+                    ship(send_own, part, v * QUAD + q)
+
             return carry
 
-        lax.fori_loop(0, q + 1, one_send, 0)
-        return carry
-
-    lax.fori_loop(0, QUAD, far_quarter, 0)
-
-    def near_quarter(j, carry):
-        q = (my_q + j) % QUAD
-        pair_of(near, near_col, 0, 128, send_near, q)
-
-        def one_send(k, carry):
-            v = (my_v + k) % WIN
-
-            @pl.when(v + q < WIN - 1)
-            def _():
-                ship(send_near, v * QUAD + q)
+        return lax.fori_loop(0, 3, early_quarter, carry)
+
+    lax.fori_loop(0, 2, early_part, 0)
+
+    def late_part(part, carry):
+        def late_quarter(j, carry):
+            q = (my_q + j) % QUAD
+
+            def one_send(k, carry):
+                to = (WIN - 1 - k) * QUAD + q
+                far_copy(part, to).wait_recv()
+
+                @pl.when(k == q)
+                def _():
+                    send_near[part, to] = (
+                        send_near[part, to].astype(F32) + got_far[part, to].astype(F32)
+                    ).astype(BF16)
+                    ship(send_near, part, to)
+
+                @pl.when(k != q)
+                def _():
+                    ship(got_far, part, to)
+
+                return carry
+
+            return lax.fori_loop(0, q + 1, one_send, carry)
+
+        return lax.fori_loop(0, QUAD, late_quarter, carry)
+
+    def one_part(part, carry):
+        lax.fori_loop(part * (CHUNKS // 2), (part + 1) * (CHUNKS // 2), cross, 0)
+
+        def far_quarter(j, carry):
+            q = (my_q + j) % QUAD
+            packets_of(far, far_col, 128, 64, send_far, part, q)
+
+            def one_send(k, carry):
+                far_copy(part, (WIN - 1 - k) * QUAD + q).start()
+                return carry
+
+            return lax.fori_loop(0, q + 1, one_send, carry)
+
+        lax.fori_loop(0, QUAD, far_quarter, 0)
+
+        def near_quarter(j, carry):
+            q = (my_q + j) % QUAD
+            packets_of(near, near_col, 0, 128, send_near, part, q)
+
+            for far_x, far_y in FARTHEST_FIRST:
+                v = (my_v // 4 + far_x) % 2 * 4 + (my_v + far_y) % 4
+
+                @pl.when((v + q > 2) & (v + q < WIN - 1))
+                def _(v=v):
+                    ship(send_near, part, v * QUAD + q)
 
             return carry
 
-        lax.fori_loop(0, WIN, one_send, 0)
-        return carry
-
-    lax.fori_loop(0, QUAD, near_quarter, 0)
-
-    def late_quarter(j, carry):
-        q = (my_q + j) % QUAD
-
-        def one_send(k, carry):
-            to = (WIN - 1 - k) * QUAD + q
-            far_copy(to).wait_recv()
-
-            @pl.when(k == q)
-            def _():
-                send_near[to] = (send_near[to].astype(F32) + got_far[to].astype(F32)).astype(BF16)
-                ship(send_near, to)
-
-            @pl.when(k != q)
-            def _():
-                ship(got_far, to)
-
-            return carry
-
-        lax.fori_loop(0, q + 1, one_send, 0)
-        return carry
-
-    lax.fori_loop(0, QUAD, late_quarter, 0)
+        lax.fori_loop(0, QUAD, near_quarter, 0)
+        return late_part(part, carry)
+
+    lax.fori_loop(0, 2, one_part, 0)
+
 
     def drain_halo(chunk, carry):
         for way in range(2):
@@ -491,24 +530,43 @@
 
     def drain_far(q, carry):
         def one(k, carry):
-            far_copy((WIN - 1 - k) * QUAD + q).wait_send()
+            for part in range(2):
+                far_copy(part, (WIN - 1 - k) * QUAD + q).wait_send()
             return carry
 
         return lax.fori_loop(0, q + 1, one, carry)
 
     lax.fori_loop(0, QUAD, drain_far, 0)
+
     loads[6].wait()
-    own_packet(send_near).wait()
-    all_offsets().wait()
-
-    for f in range(RADIX):
-        one, two = got[2 * f].astype(F32), got[2 * f + 1].astype(F32)
-        span = slice(f * 128, (f + 1) * 128)
-        lag_lhs[:128, span] = jnp.where(wide, one, pltpu.roll(two, 64, 1)).astype(BF16)
-        lag_lhs[128:, span] = jnp.where(wide, pltpu.roll(one, 64, 1), two).astype(BF16)
-    lags = jnp.dot(lag_lhs[...], table[...], preferred_element_type=F32) * scale
-    for c in range(16):
-        out[:, c, :] = lags[c * 16 : (c + 1) * 16]
+    low64 = lax.broadcasted_iota(jnp.int32, (64, 128), 1) < 64
+    even32 = (lax.broadcasted_iota(jnp.int32, (64, 128), 1) // 32) % 2 == 0
+
+    def low_high(one, two):
+        return jnp.where(low64, one, pltpu.roll(two, 64, 1)), jnp.where(low64, pltpu.roll(one, 64, 1), two)
+
+    def even_odd(one, two):
+        return jnp.where(even32, one, pltpu.roll(two, 32, 1)), jnp.where(even32, pltpu.roll(one, 96, 1), two)
+
+    for part in range(2):
+        own_packet(send_near, part).wait()
+        all_offsets(part).wait_recv()
+        for f in range(PLANE // 4):
+            packets = [got[part, 4 * f + k].astype(F32) for k in range(4)]
+            one, three = low_high(packets[0], packets[2])
+            two, four = low_high(packets[1], packets[3])
+            span = slice(f * 128, (f + 1) * 128)
+            for k, value in enumerate(even_odd(one, two) + even_odd(three, four)):
+                lag_lhs[k * 64 : (k + 1) * 64, span] = value.astype(BF16)
+        lags = jnp.dot(lag_lhs[...], table[part * NB : (part + 1) * NB, :], preferred_element_type=F32) * scale
+        if part == 0:
+            first_lags[...] = lags
+        else:
+            lags = lags + first_lags[...]
+            for c in range(16):
+                out[:, c, :] = lags[c * 16 : (c + 1) * 16]
+    for part in range(2):
+        all_offsets(part).wait_send()
 
 
 def body(planes, raw, offsets, mask):
@@ -517,7 +575,7 @@
     far_away = pl.BlockSpec(memory_space=pltpu.HBM)
     dma = pltpu.SemaphoreType.DMA
     vmem = pltpu.VMEM
-    packets = vmem((PLANE, 128, 128), BF16)
+    packets = vmem((2, PLANE, 64, 128), BF16)
     spectra = vmem((2 * BINS * OUT_PITCH, 128), F32)
     return pl.pallas_call(
         functools.partial(main_kernel, planes, 1.0 / math.sqrt(NB * 8 * WIN)),
@@ -544,17 +602,20 @@
             packets,
             packets,
             packets,
-            vmem((256, 2 * NB), BF16),
+            packets,
+            vmem((256, NB), BF16),
+            vmem((256, LAGS), F32),
+            vmem((BINS, 128, 128), BF16),
             dma((7,)),
-            dma((HALVES + 1,)),
+            dma((HALVES + 2,)),
             dma((HALVES,)),
             dma((HALVES,)),
             dma((2, HALVES, CHUNKS)),
             dma((2, HALVES, CHUNKS)),
-            dma((1,)),
-            dma((1,)),
-            dma((PLANE,)),
-            dma((PLANE,)),
+            dma((2,)),
+            dma((2,)),
+            dma((2, PLANE)),
+            dma((2, PLANE)),
         ],
         compiler_params=pltpu.CompilerParams(
             collective_id=0, has_side_effects=True, vmem_limit_bytes=48 * 2**20

time: 51.2 us -> 47.4 us (0.926)
  the two profiles are of different devices: /device:TPU:1 before, /device:TPU:7 now
where the time goes in v5:
time: 47.4 us; the launch traced here: 47.3 us
  Pallas kernels  46.5 us (98%)
  local copies, waits for them, and re-layouts  0.8 us (2%)
    pallas_call x1, Pallas kernels, body(): pl.pallas_call(functools.partial(main_kernel, planes, 1.0 / math.sqrt(NB...  46.5 us

profile of v5, /device:TPU:7, one launch (start us, length us, event | category | flops | bytes accessed | tf_op | source)
XLA Modules:
  0.0 47.3 jit_solution(4930698613769253903)
XLA Ops:
  0.0 46.5 %main.1 = f32[16,16,512]{2,1,0:T(8,128)S(1)} custom-call(s32[8]{0:T(128)} %offsets.1, s32[16]{0:T(128)} %mask.1, bf16[8,16,4352]{2,1,0:T(8,128)(2,1)} %raw_hbm.1, f32[4,16,256]{2,1,0:T(8,128)} %constant.6.clone.tables_hbm, bf16[512,256]{1,0:T(8,128)(2,1)} %constant.7.clone.weights_hbm, bf16[2048,512]{1,0:T(8,128)(2,1)} %constant.8.clone.table_hbm), custom_call_target="tpu_custom_call" | custom-call | tf_op jit(solution)/shard_map/main/pallas_call | solution.py:580
  46.5 0.8 %copy.8 = f32[16,16,512]{2,1,0:T(8,128)} copy(f32[16,16,512]{2,1,0:T(8,128)S(1)} %main.1) | data formatting | bytes 1048576

commit v6 on v5

--- a/solution.py
+++ b/solution.py
@@ -27,6 +27,8 @@
 REL_PITCH = 40
 OUT_PITCH = 72
 SLOTS = 4
+PARTS = 2
+SIDE = 16 // (2 * PARTS)
 FARTHEST_FIRST = ((1, 2), (1, 1), (1, 3), (1, 0), (0, 2), (0, 1), (0, 3), (0, 0))
 HALVES = 2
 ROWS = 128 // HALVES
@@ -64,7 +66,7 @@
     cos, sin = np.cos(angles.astype(np.float64)), np.sin(angles.astype(np.float64))
     table = np.stack([cos, -sin], 1).astype(np.float32)
     bins = RADIX * np.arange(64)[None, :] + np.arange(RADIX)[:, None]
-    table = table[bins].reshape(RADIX, 2, 2, 16, 2, LAGS)
+    table = table[bins].reshape(RADIX, 2, PARTS, BINS // PARTS, 2, LAGS)
     return table.transpose(2, 0, 1, 3, 4, 5).reshape(2 * NB, LAGS).astype(jnp.bfloat16)
 
 
@@ -105,11 +107,14 @@
     def signal(plane, s):
         pl.semaphore_signal(barrier, inc=1, device_id=device(plane, s), device_id_type=MESH)
 
-    def near(j, carry):
-        signal(z, (me + j) % PLANE)
-        return carry
-
-    lax.fori_loop(1, PLANE, near, 0)
+    for far_x, far_y in FARTHEST_FIRST:
+        v = (me // QUAD // 4 + far_x) % 2 * 4 + (me // QUAD + far_y) % 4
+
+        def one(j, carry, v=v):
+            signal(z, v * QUAD + (me + j) % QUAD)
+            return carry
+
+        lax.fori_loop(0 if far_x + far_y else 1, QUAD, one, 0, unroll=True)
     signal((z + 1) % planes, me)
     signal((z + planes - 1) % planes, me)
     return PLANE - 1 + 2
@@ -239,9 +244,11 @@
     ] + [(tables_hbm, tables), (weights_hbm, weights), (table_hbm, table)]
     pairs = [pairs[i] for i in (4, 0, 1, 2, 3, 5, 6)]
     loads = [pltpu.make_async_copy(source, target, in_sem.at[i]) for i, (source, target) in enumerate(pairs)]
-    for load in loads[:6]:
+    for load in loads[:3]:
         load.start()
     expected = greet_all(planes, z, me)
+    for load in loads[3:6]:
+        load.start()
     shifts(offsets, turn_f, turn_g)
     for slot in range(SLOTS):
         near_col[slot, 128:, :] = jnp.zeros((128, 128), F32)
@@ -286,6 +293,8 @@
             top, bottom = value[:32], value[32:]
             send[half, 2 * f] = jnp.where(left[:32], top, pltpu.roll(bottom, 64, 1)).astype(BF16)
             send[half, 2 * f + 1] = jnp.where(left[:32], pltpu.roll(top, 64, 1), bottom).astype(BF16)
+        if half:
+            all_bins(half - 1).wait_send()
         own_copy(half).start()
 
         for far_x, far_y in FARTHEST_FIRST:
@@ -296,8 +305,6 @@
                 return carry
 
             lax.fori_loop(0 if far_x + far_y else 1, QUAD, launch, 0)
-
-    loads[6].start()
 
     def halo_copy(way, half, chunk):
         span = pl.ds(chunk * CHUNK, CHUNK)
@@ -337,8 +344,7 @@
 
         lax.fori_loop(0, CHUNKS, gather, 0)
 
-    for half in range(HALVES):
-        all_bins(half).wait_send()
+    all_bins(HALVES - 1).wait_send()
 
     def operand(x, rx):
         def turn(u):
@@ -429,21 +435,26 @@
     def packets_of(ref, column, base, size, target, part, q):
         def one_group(i, carry):
             c = q * 16 + i
-            start = part * BINS * OUT_PITCH
+            start = part * (2 * BINS // PARTS) * OUT_PITCH
             block = jnp.concatenate(
-                [ref[pl.ds(start + c + 4 * k, BINS, stride=OUT_PITCH), :] for k in range(4)], 0
+                [
+                    ref[pl.ds(start + c + SIDE * k, 2 * BINS // PARTS, stride=OUT_PITCH), :]
+                    for k in range(2 * PARTS)
+                ],
+                0,
             )
             column[i, base : base + size, :] = block.T[:size]
-            value = column[i, pl.ds(c + 13, 128), :]
-            for k in (2, 1, 0):
-                value = jnp.where(lane < 32 * k + 32, column[i, pl.ds(c + 4 * k + 1, 128), :], value)
+            value = column[i, pl.ds(c + SIDE * (2 * PARTS - 1) + 1, 128), :]
+            for k in reversed(range(2 * PARTS - 1)):
+                here = column[i, pl.ds(c + SIDE * k + 1, 128), :]
+                value = jnp.where(lane < (k + 1) * (2 * BINS // PARTS), here, value)
             value = value.astype(BF16)
             rows = pl.ds(pl.multiple_of(i * 16, 16), 16)
             for v in range(WIN):
                 target[part, v * QUAD + q, rows, :] = value[v * 16 : (v + 1) * 16]
             return carry
 
-        lax.fori_loop(0, 4, one_group, 0, unroll=4)
+        lax.fori_loop(0, SIDE, one_group, 0, unroll=True)
 
     def early_part(part, carry):
         def early_quarter(q, carry):
@@ -459,7 +470,8 @@
 
         return lax.fori_loop(0, 3, early_quarter, carry)
 
-    lax.fori_loop(0, 2, early_part, 0)
+    lax.fori_loop(0, PARTS, early_part, 0)
+    loads[6].start()
 
     def late_part(part, carry):
         def late_quarter(j, carry):
@@ -487,7 +499,7 @@
         return lax.fori_loop(0, QUAD, late_quarter, carry)
 
     def one_part(part, carry):
-        lax.fori_loop(part * (CHUNKS // 2), (part + 1) * (CHUNKS // 2), cross, 0)
+        lax.fori_loop(part * (CHUNKS // PARTS), (part + 1) * (CHUNKS // PARTS), cross, 0)
 
         def far_quarter(j, carry):
             q = (my_q + j) % QUAD
@@ -517,7 +529,7 @@
         lax.fori_loop(0, QUAD, near_quarter, 0)
         return late_part(part, carry)
 
-    lax.fori_loop(0, 2, one_part, 0)
+    lax.fori_loop(0, PARTS, one_part, 0)
 
 
     def drain_halo(chunk, carry):
@@ -530,7 +542,7 @@
 
     def drain_far(q, carry):
         def one(k, carry):
-            for part in range(2):
+            for part in range(PARTS):
                 far_copy(part, (WIN - 1 - k) * QUAD + q).wait_send()
             return carry
 
@@ -539,33 +551,41 @@
     lax.fori_loop(0, QUAD, drain_far, 0)
 
     loads[6].wait()
-    low64 = lax.broadcasted_iota(jnp.int32, (64, 128), 1) < 64
-    even32 = (lax.broadcasted_iota(jnp.int32, (64, 128), 1) // 32) % 2 == 0
-
-    def low_high(one, two):
-        return jnp.where(low64, one, pltpu.roll(two, 64, 1)), jnp.where(low64, pltpu.roll(one, 64, 1), two)
-
-    def even_odd(one, two):
-        return jnp.where(even32, one, pltpu.roll(two, 32, 1)), jnp.where(even32, pltpu.roll(one, 96, 1), two)
-
-    for part in range(2):
+    row_lane = lax.broadcasted_iota(jnp.int32, (SIDE * 16, 128), 1)
+
+    def swap(one, two, width):
+        even = (row_lane // width) % 2 == 0
+        return (
+            jnp.where(even, one, pltpu.roll(two, width, 1)),
+            jnp.where(even, pltpu.roll(one, 128 - width, 1), two),
+        )
+
+    count = 2 * PARTS
+    depth = 2 * NB // PARTS
+    for part in range(PARTS):
         own_packet(send_near, part).wait()
         all_offsets(part).wait_recv()
-        for f in range(PLANE // 4):
-            packets = [got[part, 4 * f + k].astype(F32) for k in range(4)]
-            one, three = low_high(packets[0], packets[2])
-            two, four = low_high(packets[1], packets[3])
-            span = slice(f * 128, (f + 1) * 128)
-            for k, value in enumerate(even_odd(one, two) + even_odd(three, four)):
-                lag_lhs[k * 64 : (k + 1) * 64, span] = value.astype(BF16)
-        lags = jnp.dot(lag_lhs[...], table[part * NB : (part + 1) * NB, :], preferred_element_type=F32) * scale
-        if part == 0:
-            first_lags[...] = lags
-        else:
-            lags = lags + first_lags[...]
-            for c in range(16):
-                out[:, c, :] = lags[c * 16 : (c + 1) * 16]
-    for part in range(2):
+        for f in range(PLANE // count):
+            blocks = [got[part, count * f + k].astype(F32) for k in range(count)]
+            step = count // 2
+            while step:
+                for k in range(count):
+                    if not k & step:
+                        blocks[k], blocks[k + step] = swap(blocks[k], blocks[k + step], step * (128 // count))
+                step //= 2
+            span = slice(part * depth + f * 128, part * depth + (f + 1) * 128)
+            for k in range(count):
+                lag_lhs[k * SIDE * 16 : (k + 1) * SIDE * 16, span] = blocks[k].astype(BF16)
+        if part == PARTS - 2:
+            first_lags[...] = jnp.dot(
+                lag_lhs[:, : (part + 1) * depth], table[: (part + 1) * depth, :], preferred_element_type=F32
+            )
+    last = (PARTS - 1) * depth
+    lags = jnp.dot(lag_lhs[:, last:], table[last:, :], preferred_element_type=F32)
+    lags = (lags + first_lags[...]) * scale
+    for c in range(16):
+        out[:, c, :] = lags[c * 16 : (c + 1) * 16]
+    for part in range(PARTS):
         all_offsets(part).wait_send()
 
 
@@ -575,8 +595,8 @@
     far_away = pl.BlockSpec(memory_space=pltpu.HBM)
     dma = pltpu.SemaphoreType.DMA
     vmem = pltpu.VMEM
-    packets = vmem((2, PLANE, 64, 128), BF16)
-    spectra = vmem((2 * BINS * OUT_PITCH, 128), F32)
+    packets = vmem((PARTS, PLANE, SIDE * 16, 128), BF16)
+    spectra = vmem(((2 * BINS + 1) * OUT_PITCH, 128), F32)
     return pl.pallas_call(
         functools.partial(main_kernel, planes, 1.0 / math.sqrt(NB * 8 * WIN)),
         out_shape=jax.ShapeDtypeStruct((16, 16, LAGS), F32),
@@ -591,7 +611,7 @@
             vmem((ROWS // 16, 16, 128), F32),
             vmem((HALVES, PLANE, 32, 128), BF16),
             vmem((HALVES, PLANE, 32, 128), BF16),
-            vmem((64 * REL_PITCH, 128), F32),
+            vmem((65 * REL_PITCH, 128), F32),
             vmem((HALVES, BINS, 32, 128), BF16),
             vmem((2, HALVES, BINS, 32, 128), BF16),
             spectra,
@@ -603,19 +623,19 @@
             packets,
             packets,
             packets,
-            vmem((256, NB), BF16),
+            vmem((256, 2 * NB), BF16),
             vmem((256, LAGS), F32),
             vmem((BINS, 128, 128), BF16),
             dma((7,)),
-            dma((HALVES + 2,)),
+            dma((HALVES + PARTS,)),
             dma((HALVES,)),
             dma((HALVES,)),
             dma((2, HALVES, CHUNKS)),
             dma((2, HALVES, CHUNKS)),
-            dma((2,)),
-            dma((2,)),
-            dma((2, PLANE)),
-            dma((2, PLANE)),
+            dma((PARTS,)),
+            dma((PARTS,)),
+            dma((PARTS, PLANE)),
+            dma((PARTS, PLANE)),
         ],
         compiler_params=pltpu.CompilerParams(
             collective_id=0, has_side_effects=True, vmem_limit_bytes=48 * 2**20

time: 47.4 us -> 47.3 us (level)
  no operation moved by 1% of the time
where the time goes in v6:
time: 47.3 us; the launch traced here: 47.2 us
  Pallas kernels  46.4 us (98%)
  local copies, waits for them, and re-layouts  0.8 us (2%)
    pallas_call x1, Pallas kernels, body(): pl.pallas_call(functools.partial(main_kernel, planes, 1.0 / math.sqrt(NB...  46.4 us

profile of v6, /device:TPU:7, one launch (start us, length us, event | category | flops | bytes accessed | tf_op | source)
XLA Modules:
  0.0 47.2 jit_solution(9289820432721322622)
XLA Ops:
  0.0 46.4 %main.1 = f32[16,16,512]{2,1,0:T(8,128)S(1)} custom-call(s32[8]{0:T(128)} %offsets.1, s32[16]{0:T(128)} %mask.1, bf16[8,16,4352]{2,1,0:T(8,128)(2,1)} %raw_hbm.1, f32[4,16,256]{2,1,0:T(8,128)} %constant.6.clone.tables_hbm, bf16[512,256]{1,0:T(8,128)(2,1)} %constant.7.clone.weights_hbm, bf16[2048,512]{1,0:T(8,128)(2,1)} %constant.8.clone.table_hbm), custom_call_target="tpu_custom_call" | custom-call | tf_op jit(solution)/shard_map/main/pallas_call | solution.py:600
  46.4 0.8 %copy.8 = f32[16,16,512]{2,1,0:T(8,128)} copy(f32[16,16,512]{2,1,0:T(8,128)S(1)} %main.1) | data formatting | bytes 1048576

commit v7 on v6

--- a/solution.py
+++ b/solution.py
@@ -255,6 +255,24 @@
         far_col[slot, :128, :] = jnp.zeros((128, 128), F32)
     left = lax.broadcasted_iota(jnp.int32, (64, 128), 1) < 64
 
+    def at_ends(down, up, do):
+        @pl.when(z > 0)
+        def _():
+            do(down)
+
+        @pl.when(z + 1 < planes)
+        def _():
+            do(up)
+
+    @pl.when(z + 1 == planes)
+    def _():
+        def clear(to, carry):
+            for part in range(PARTS):
+                got_far[part, to] = jnp.zeros((SIDE * 16, 128), BF16)
+            return carry
+
+        lax.fori_loop(0, PLANE, clear, 0)
+
     def bins_copy(half, to, source):
         return pltpu.make_async_remote_copy(
             src_ref=send.at[half, to],
@@ -338,8 +356,7 @@
                 real = turned[pl.ds(half * 32 * REL_PITCH + g, 16, stride=REL_PITCH), :]
                 imag = turned[pl.ds((half * 32 + 16) * REL_PITCH + g, 16, stride=REL_PITCH), :]
                 own[half, g] = jnp.concatenate([real, imag], 0).astype(BF16)
-            halo_copy(0, half, chunk).start()
-            halo_copy(1, half, chunk).start()
+            at_ends(0, 1, lambda way: halo_copy(way, half, chunk).start())
             return carry
 
         lax.fori_loop(0, CHUNKS, gather, 0)
@@ -371,9 +388,8 @@
     lax.fori_loop(0, BINS, own_operand, 0, unroll=4)
 
     def cross(chunk, carry):
-        for way in range(2):
-            for half in range(HALVES):
-                halo_copy(way, half, chunk).wait_recv()
+        for half in range(HALVES):
+            at_ends(1, 0, lambda way, half=half: halo_copy(way, half, chunk).wait_recv())
         for j in range(CHUNK):
             g = chunk * CHUNK + j
             a = own_rows(g)
@@ -479,7 +495,11 @@
 
             def one_send(k, carry):
                 to = (WIN - 1 - k) * QUAD + q
-                far_copy(part, to).wait_recv()
+
+                @pl.when(z + 1 < planes)
+                def _():
+                    far_copy(part, to).wait_recv()
+
 
                 @pl.when(k == q)
                 def _():
@@ -506,7 +526,11 @@
             packets_of(far, far_col, 128, 64, send_far, part, q)
 
             def one_send(k, carry):
-                far_copy(part, (WIN - 1 - k) * QUAD + q).start()
+
+                @pl.when(z > 0)
+                def _():
+                    far_copy(part, (WIN - 1 - k) * QUAD + q).start()
+
                 return carry
 
             return lax.fori_loop(0, q + 1, one_send, carry)
@@ -533,9 +557,8 @@
 
 
     def drain_halo(chunk, carry):
-        for way in range(2):
-            for half in range(HALVES):
-                halo_copy(way, half, chunk).wait_send()
+        for half in range(HALVES):
+            at_ends(0, 1, lambda way, half=half: halo_copy(way, half, chunk).wait_send())
         return carry
 
     lax.fori_loop(0, CHUNKS, drain_halo, 0)
@@ -548,7 +571,10 @@
 
         return lax.fori_loop(0, q + 1, one, carry)
 
-    lax.fori_loop(0, QUAD, drain_far, 0)
+    @pl.when(z > 0)
+    def _():
+        lax.fori_loop(0, QUAD, drain_far, 0)
+
 
     loads[6].wait()
     row_lane = lax.broadcasted_iota(jnp.int32, (SIDE * 16, 128), 1)

time: 47.3 us -> 46.1 us (0.975)
  the two profiles are of different devices: /device:TPU:7 before, /device:TPU:71 now
where the time goes in v7:
time: 46.1 us; the launch traced here: 46 us
  Pallas kernels  45.2 us (98%)
  local copies, waits for them, and re-layouts  0.8 us (2%)
    pallas_call x1, Pallas kernels, body(): pl.pallas_call(functools.partial(main_kernel, planes, 1.0 / math.sqrt(NB...  45.2 us

profile of v7, /device:TPU:71, one launch (start us, length us, event | category | flops | bytes accessed | tf_op | source)
XLA Modules:
  0.0 46.0 jit_solution(4710465210795368053)
XLA Ops:
  0.0 45.2 %main.1 = f32[16,16,512]{2,1,0:T(8,128)S(1)} custom-call(s32[8]{0:T(128)} %offsets.1, s32[16]{0:T(128)} %mask.1, bf16[8,16,4352]{2,1,0:T(8,128)(2,1)} %raw_hbm.1, f32[4,16,256]{2,1,0:T(8,128)} %constant.6.clone.tables_hbm, bf16[512,256]{1,0:T(8,128)(2,1)} %constant.7.clone.weights_hbm, bf16[2048,512]{1,0:T(8,128)(2,1)} %constant.8.clone.table_hbm), custom_call_target="tpu_custom_call" | custom-call | tf_op jit(solution)/shard_map/main/pallas_call | solution.py:626
  45.2 0.8 %copy.8 = f32[16,16,512]{2,1,0:T(8,128)} copy(f32[16,16,512]{2,1,0:T(8,128)S(1)} %main.1) | data formatting | bytes 1048576

commit v8 on v7

--- a/solution.py
+++ b/solution.py
@@ -115,9 +115,16 @@
             return carry
 
         lax.fori_loop(0 if far_x + far_y else 1, QUAD, one, 0, unroll=True)
-    signal((z + 1) % planes, me)
-    signal((z + planes - 1) % planes, me)
-    return PLANE - 1 + 2
+
+    @pl.when(z + 1 < planes)
+    def _():
+        signal((z + 1) % planes, me)
+
+    @pl.when(z > 0)
+    def _():
+        signal((z + planes - 1) % planes, me)
+
+    return PLANE - 1 + jnp.where(z > 0, 1, 0) + jnp.where(z + 1 < planes, 1, 0)
 
 
 def window_of(half, i):

time: 46.1 us -> 46.1 us (level)
  no operation moved by 1% of the time
where the time goes in v8:
time: 46.1 us; the launch traced here: 46 us
  Pallas kernels  45.2 us (98%)
  local copies, waits for them, and re-layouts  0.8 us (2%)
    pallas_call x1, Pallas kernels, body(): pl.pallas_call(functools.partial(main_kernel, planes, 1.0 / math.sqrt(NB...  45.2 us

profile of v8, /device:TPU:71, one launch (start us, length us, event | category | flops | bytes accessed | tf_op | source)
XLA Modules:
  0.0 46.0 jit_solution(7952468547398933210)
XLA Ops:
  0.0 45.2 %main.1 = f32[16,16,512]{2,1,0:T(8,128)S(1)} custom-call(s32[8]{0:T(128)} %offsets.1, s32[16]{0:T(128)} %mask.1, bf16[8,16,4352]{2,1,0:T(8,128)(2,1)} %raw_hbm.1, f32[4,16,256]{2,1,0:T(8,128)} %constant.6.clone.tables_hbm, bf16[512,256]{1,0:T(8,128)(2,1)} %constant.7.clone.weights_hbm, bf16[2048,512]{1,0:T(8,128)(2,1)} %constant.8.clone.table_hbm), custom_call_target="tpu_custom_call" | custom-call | tf_op jit(solution)/shard_map/main/pallas_call | solution.py:633
  45.2 0.8 %copy.8 = f32[16,16,512]{2,1,0:T(8,128)} copy(f32[16,16,512]{2,1,0:T(8,128)S(1)} %main.1) | data formatting | bytes 1048576
